TPU v7x, 128 devices: a whole 4x4x4 slice. The times are simulated.
128 devices in a mesh: rep: 16 (over x, z), tp: 8 (over y, core).
Axes of the slice: x: 4, y: 4, z: 4, core: 2. Of those that a mesh axis runs over, the one named last changes fastest.
Arguments:
- tokens: bfloat16 [768, 16384], P(None, ('rep', 'tp')), may hold values from -6 to 6
- gate_weight: bfloat16 [16384, 26624], P(('rep', 'tp')), may hold values from -1 to 1
- up_weight: bfloat16 [16384, 26624], P(('rep', 'tp')), may hold values from -1 to 1
- down_weight: bfloat16 [26624, 16384], P(None, ('rep', 'tp')), may hold values from -1 to 1
Outputs:
- output_block: bfloat16 [768, 16384], P(None, ('rep', 'tp'))
- peak_values: float32 [3], replicated
All inputs are finite; a program needn't handle non-finite values. Where the computation divides by a largest or mean magnitude, that divisor is 1e-20 or more.
Results may differ from a plain program's by a relative error of at most 0.0051.
Values may be sent and summed in bfloat16 or wider, within the bound.
A program may use at most 192 MiB of HBM per device.

v0:
```python
import jax
import jax.numpy as jnp
from jax import lax
from jax.sharding import PartitionSpec as P


def local_peaks(first, second, third):
    return jnp.stack(
        [
            jnp.max(jnp.abs(first)).astype(jnp.float32),
            jnp.max(jnp.abs(second)).astype(jnp.float32),
            jnp.max(jnp.abs(third)).astype(jnp.float32),
        ]
    )


def scaled_copy(weight, peak_value):
    factor = 127.0 / peak_value
    return jnp.floor(weight.astype(jnp.float32) * factor + 0.5).astype(jnp.bfloat16)


def shards(tokens, gate_weight, up_weight, down_weight):
    gate_cols, up_cols = (
        lax.all_to_all(gate_weight, "rep", split_axis=1, concat_axis=0, tiled=True),
        lax.all_to_all(up_weight, "rep", split_axis=1, concat_axis=0, tiled=True),
    )
    down_rows = lax.all_to_all(down_weight, "rep", split_axis=0, concat_axis=1, tiled=True)
    peak_values = lax.pmax(local_peaks(gate_cols, up_cols, down_rows), ("rep", "tp"))
    features_all = lax.all_gather(tokens, "rep", axis=1, tiled=True)
    gate_part = jnp.dot(
        features_all, scaled_copy(gate_cols, peak_values[0]), preferred_element_type=jnp.float32
    ) * (peak_values[0] / 127.0)
    up_part = jnp.dot(
        features_all, scaled_copy(up_cols, peak_values[1]), preferred_element_type=jnp.float32
    ) * (peak_values[1] / 127.0)
    gate_sum, up_sum = lax.psum((gate_part, up_part), "tp")
    hidden = (jax.nn.silu(gate_sum) * up_sum).astype(jnp.bfloat16)
    partial_out = jnp.dot(
        hidden, scaled_copy(down_rows, peak_values[2]), preferred_element_type=jnp.float32
    ) * (peak_values[2] / 127.0)
    output_block = lax.psum_scatter(partial_out, "rep", scatter_dimension=1, tiled=True).astype(
        jnp.bfloat16
    )
    return (output_block, peak_values)


def solution(mesh):
    in_specs = (
        P(None, ("rep", "tp")),
        P(("rep", "tp"), None),
        P(("rep", "tp"), None),
        P(None, ("rep", "tp")),
    )
    out_specs = (P(None, ("rep", "tp")), P())
    return jax.shard_map(shards, mesh=mesh, in_specs=in_specs, out_specs=out_specs, check_vma=False)
```

profile of v0, /device:TPU:1, one launch (start us, length us, event | category | flops | bytes accessed | tf_op | source)
XLA Modules:
  0.0 666.7 jit_solution(16810718787113933693)
XLA Ops:
  7.2 10.0 %copy.6 = bf16[128,26624]{0,1:T(8,128)(2,1)} copy(bf16[128,26624]{1,0:T(8,128)(2,1)} %param.5) | data formatting | bytes 13631488 | tf_op args[1]
  17.1 8.5 %all-to-all-start = ((bf16[128,16,1664]{0,2,1:T(8,128)(2,1)}), bf16[128,16,1664]{0,2,1:T(8,128)(2,1)}, u32[]{:S(2)}, u32[]{:S(2)}) async-start(bf16[128,16,1664]{0,2,1:T(8,128)(2,1)} %bitcast.30), calls=%async_computation | async-start | bytes 13631488 | tf_op jit(solution)/shard_map/all_to_all | solution.py:24
  25.6 9.9 %copy.7 = bf16[128,26624]{0,1:T(8,128)(2,1)} copy(bf16[128,26624]{1,0:T(8,128)(2,1)} %param.6) | data formatting | bytes 13631488 | tf_op args[2]
  35.5 103.8 %all-to-all-done = bf16[128,16,1664]{0,2,1:T(8,128)(2,1)} async-done(((bf16[128,16,1664]{0,2,1:T(8,128)(2,1)}), bf16[128,16,1664]{0,2,1:T(8,128)(2,1)}, u32[]{:S(2)}, u32[]{:S(2)}) %all-to-all-start) | async-done | bytes 6815776 | tf_op jit(solution)/shard_map/all_to_all | solution.py:24
  139.3 83.7 %all_to_all.39 = bf16[128,16,1664]{0,2,1:T(8,128)(2,1)} all-to-all(bf16[128,16,1664]{0,2,1:T(8,128)(2,1)} %bitcast.31), channel_id=1, replica_groups=mesh['rep'=16,'tp'=8] {'rep'}, dimensions={1} | all-to-all | bytes 13631488 | tf_op jit(solution)/shard_map/all_to_all | solution.py:25
  223.0 4.7 all-to-all-start.2
  228.5 4.6 abs_reduce_fusion.2
  233.4 1.5 abs_reduce_fusion.1
  234.8 74.6 %all-to-all-done.2 = bf16[16,1664,128]{2,1,0:T(8,128)(2,1)} async-done(((bf16[16,1664,128]{2,1,0:T(8,128)(2,1)}), bf16[16,1664,128]{2,1,0:T(8,128)(2,1)}, u32[]{:S(2)}, u32[]{:S(2)}) %all-to-all-start.2) | async-done | bytes 6815776 | tf_op jit(solution)/shard_map/all_to_all | solution.py:27
  309.4 4.4 abs_reduce_fusion
  313.9 2.0 maximum_convert_fusion
  315.8 71.4 %pmax.7 = f32[3]{0:T(128)S(1)} all-reduce(f32[3]{0:T(128)S(1)} %maximum_convert_fusion), channel_id=1, replica_groups=mesh['rep'=16,'tp'=8] {'rep','tp'}, use_global_device_ids=true, to_apply=%region_3.0 | all-reduce | flops 3 | bytes 24 | tf_op jit(solution)/shard_map/pmax | solution.py:28
  390.6 8.2 %fusion = bf16[16,128,1664]{1,2,0:T(8,128)(2,1)} fusion(bf16[128,16,1664]{0,2,1:T(8,128)(2,1)} %all-to-all-done, f32[]{:T(128)} %bitcast.6), kind=kLoop, calls=%fused_computation.3 | loop fusion | flops 17039360 | bytes 13631492 | tf_op jit(solution)/shard_map/convert.6
  398.8 9.8 %copy.8 = bf16[16,128,1664]{2,1,0:T(8,128)(2,1)} copy(bf16[16,128,1664]{1,2,0:T(8,128)(2,1)} %fusion) | data formatting | bytes 13631488 | tf_op jit(solution)/shard_map/convert.6
  408.6 8.1 %fusion.1 = bf16[16,128,1664]{1,2,0:T(8,128)(2,1)} fusion(bf16[128,16,1664]{0,2,1:T(8,128)(2,1)} %all_to_all.39, f32[]{:T(128)} %bitcast.11), kind=kLoop, calls=%fused_computation.4 | loop fusion | flops 17039360 | bytes 13631492 | tf_op jit(solution)/shard_map/convert.5
  416.7 9.8 %copy.9 = bf16[16,128,1664]{2,1,0:T(8,128)(2,1)} copy(bf16[16,128,1664]{1,2,0:T(8,128)(2,1)} %fusion.1) | data formatting | bytes 13631488 | tf_op jit(solution)/shard_map/convert.5
  426.5 11.9 %multiply_bitcast_fusion.1 = f32[768,1664]{0,1:T(8,128)} fusion(bf16[2048,1664]{1,0:T(8,128)(2,1)} %bitcast.34, bf16[768,2048]{1,0:T(8,128)(2,1)} %all-gather.2.cloned.1.call-done, f32[]{:T(128)} %bitcast.9), kind=kOutput, calls=%fused_computation.11 | convolution fusion | flops 5235769344 | bytes 15073284 | tf_op jit(solution)/shard_map/dot_general | solution.py:30
  438.4 8.0 %multiply_bitcast_fusion = f32[768,1664]{0,1:T(8,128)} fusion(bf16[2048,1664]{1,0:T(8,128)(2,1)S(1)} %bitcast.35, bf16[768,2048]{1,0:T(8,128)(2,1)S(1)} %copy-done.3, f32[]{:T(128)} %bitcast.14), kind=kOutput, calls=%fused_computation.10 | convolution fusion | flops 5235769344 | bytes 15073284 | tf_op jit(solution)/shard_map/dot_general | solution.py:33
  448.0 8.1 %fusion.2 = bf16[1664,16,128]{2,0,1:T(8,128)(2,1)} fusion(bf16[16,1664,128]{2,1,0:T(8,128)(2,1)} %all-to-all-done.2, f32[]{:T(128)} %bitcast.16), kind=kLoop, calls=%fused_computation.5 | loop fusion | flops 17039360 | bytes 13631492 | tf_op jit(solution)/shard_map/convert.4
  456.1 9.9 %copy.10 = bf16[1664,16,128]{0,2,1:T(8,128)(2,1)} copy(bf16[1664,16,128]{2,0,1:T(8,128)(2,1)} %fusion.2) | data formatting | bytes 13631488 | tf_op jit(solution)/shard_map/convert.4
  466.0 98.8 %all-reduce.3.cloned.1.call-done = (f32[768,1664]{0,1:T(8,128)}, f32[768,1664]{0,1:T(8,128)}) async-done(((f32[768,1664]{0,1:T(8,128)}, f32[768,1664]{0,1:T(8,128)}), (f32[768,1664]{0,1:T(8,128)}, f32[768,1664]{0,1:T(8,128)})) %all-reduce.3.cloned.1.call-update) | async-done | bytes 10223632 | tf_op jit(solution)/shard_map/psum | solution.py:36
  564.8 12.9 %convolution_multiply_fusion = f32[768,2048]{1,0:T(8,128)} fusion(bf16[1664,2048]{0,1:T(8,128)(2,1)} %bitcast.33, f32[]{:T(128)} %bitcast.19, f32[768,1664]{0,1:T(8,128)} %get-tuple-element.2, f32[768,1664]{0,1:T(8,128)} %get-tuple-element.3), kind=kOutput, calls=%fused_computation.12 | convolution fusion | flops 5243731968 | bytes 23330820 | tf_op jit(solution)/shard_map/dot_general | solution.py:38
  577.7 80.7 %reduce-scatter.2.cloned.1.call-done = f32[768,128]{1,0:T(8,128)} async-done(((f32[768,2048]{1,0:T(8,128)}), f32[768,128]{1,0:T(8,128)}) %reduce-scatter.2.cloned.1.call-update) | async-done | bytes 393232 | tf_op jit(solution)/shard_map/reduce_scatter | solution.py:41
  658.5 1.7 convert_element_type.31
  (16 shorter events, 2.0 us)
Async XLA Ops:
  17.1 122.2 %all-to-all-start = ((bf16[128,16,1664]{0,2,1:T(8,128)(2,1)}), bf16[128,16,1664]{0,2,1:T(8,128)(2,1)}, u32[]{:S(2)}, u32[]{:S(2)}) async-start(bf16[128,16,1664]{0,2,1:T(8,128)(2,1)} %bitcast.30), calls=%async_computation | async-start | bytes 13631488 | tf_op jit(solution)/shard_map/all_to_all | solution.py:24
  223.0 86.4 %all-to-all-start.2 = ((bf16[16,1664,128]{2,1,0:T(8,128)(2,1)}), bf16[16,1664,128]{2,1,0:T(8,128)(2,1)}, u32[]{:S(2)}, u32[]{:S(2)}) async-start(bf16[16,1664,128]{2,1,0:T(8,128)(2,1)} %bitcast.32), calls=%async_computation.2 | async-start | bytes 13631488 | tf_op jit(solution)/shard_map/all_to_all | solution.py:27
  227.7 198.8 %all-gather.2.cloned.1.call-start = ((), (), s32[]{:S(2)}) async-start(), calls=%async_computation.4 | async-start | bytes 3342336 | tf_op jit(solution)/shard_map/all_gather | solution.py:29
  228.4 336.4 %all-reduce.3.cloned.1.call-start = ((), (), s32[]{:S(2)}) async-start(), calls=%async_computation.6 | async-start | bytes 20447232 | tf_op jit(solution)/shard_map/psum | solution.py:36
  228.5 4.9 copy-start
  387.3 11.6 %copy-start.2 = (f32[3]{0:T(128)}, f32[3]{0:T(128)S(1)}, u32[]{:S(2)}) copy-start(f32[3]{0:T(128)S(1)} %pmax.7) | copy-start | bytes 40
  426.5 11.9 %copy-start.1 = (bf16[16,128,1664]{2,1,0:T(8,128)(2,1)S(1)}, bf16[16,128,1664]{2,1,0:T(8,128)(2,1)}, u32[]{:S(2)}) copy-start(bf16[16,128,1664]{2,1,0:T(8,128)(2,1)} %copy.9) | copy-start | bytes 20447236
  426.5 11.9 %copy-start.3 = (bf16[768,2048]{1,0:T(8,128)(2,1)S(1)}, bf16[768,2048]{1,0:T(8,128)(2,1)}, u32[]{:S(2)}) copy-start(bf16[768,2048]{1,0:T(8,128)(2,1)} %all-gather.2.cloned.1.call-done) | copy-start | bytes 9437188
  446.4 212.0 %reduce-scatter.2.cloned.1.call-start = ((), (), s32[]{:S(2)}) async-start(), calls=%async_computation.5 | async-start | bytes 6684672 | tf_op jit(solution)/shard_map/reduce_scatter | solution.py:41
Sparse Core Ops, SparseCore 0:
  230.7 115.4 all-gather.1
  446.5 118.2 all-reduce.2
  577.9 80.5 reduce-scatter.1
where the time goes:
time: 669 us; the launch traced here: 667 us
  waiting for transfers between devices  359 us (54%)
  blocking collectives  155 us (23%)
  local copies, waits for them, and re-layouts  50.3 us (8%)
  other arithmetic  38.6 us (6%)
  matrix products  32.7 us (5%)
  between operations  17.8 us (3%)
  starting transfers between devices  13.5 us (2%)
    all_to_all x1, waiting for transfers between devices, shards(): lax.all_to_all(gate_weight, 'rep', split_axis=1, concat_axis=0, tiled=True)  104 us
    psum x1, waiting for transfers between devices, shards(): gate_sum, up_sum = lax.psum((gate_part, up_part), 'tp')  98.8 us
    all_to_all x1, blocking collectives, shards(): lax.all_to_all(up_weight, 'rep', split_axis=1, concat_axis=0, tiled=True)  83.7 us
    reduce_scatter x1, waiting for transfers between devices, shards(): lax.psum_scatter(partial_out, 'rep', scatter_dimension=1, tiled=True)  80.7 us
    all_to_all x1, waiting for transfers between devices, shards(): lax.all_to_all(down_weight, 'rep', split_axis=0, concat_axis=1, tiled=True)  74.6 us
    pmax x1, blocking collectives, shards(): lax.pmax(local_peaks(gate_cols, up_cols, down_rows), ('rep', 'tp'))  71.4 us
    another operation x3, local copies, waits for them, and re-layouts  29.5 us
    another operation x3, other arithmetic  24.4 us
  transfers between devices with their start and end apart: 5, of which 4 were waited for; matrix products, arithmetic and copies ran while one was open for 12% of the time, Pallas kernels for 0%

commit v1 on v0

v1 whole, which is shorter than its diff:
```python
import functools

import jax
import jax.numpy as jnp
from jax import lax
from jax.experimental import pallas as pl
from jax.experimental.pallas import tpu as pltpu
from jax.sharding import PartitionSpec as P

MESH = pl.DeviceIdType.MESH
SIDE = 4
SUM_AXES = ((1, 2), (2, 0), (0, 1))


def class_widths(ff):
    units = ff // (8 * 128)
    first = (units + 2) // 3
    second = (units - first + 1) // 2
    return [first * 128, second * 128, (units - first - second) * 128]


def class_bases(widths):
    return [0, 8 * widths[0], 8 * (widths[0] + widths[1])]


def place():
    rep = lax.axis_index("rep")
    tp = lax.axis_index("tp")
    return (rep // SIDE, tp // 2, lax.rem(rep, SIDE)), lax.rem(tp, 2)


def device_at(xyz, core):
    return (xyz[0] * SIDE + xyz[2], xyz[1] * 2 + core)


def moved(xyz, axis, step):
    out = list(xyz)
    out[axis] = lax.rem(xyz[axis] + step, SIDE)
    return tuple(out)


def mult(value, of):
    return pl.multiple_of(value, of)


class Mail:
    def __init__(self, send_sems, recv_sems):
        self.send_sems, self.recv_sems, self.used, self.sent = send_sems, recv_sems, 0, []

    def post(self, src, dst, device):
        copy = pltpu.make_async_remote_copy(
            src_ref=src,
            dst_ref=dst,
            send_sem=self.send_sems.at[self.used],
            recv_sem=self.recv_sems.at[self.used],
            device_id=device,
            device_id_type=MESH,
        )
        self.used += 1
        copy.start()
        self.sent.append(copy)
        return copy

    def finish(self):
        for copy in self.sent:
            copy.wait_send()


def greet(partners):
    barrier = pltpu.get_barrier_semaphore()
    for partner in partners:
        pl.semaphore_signal(barrier, inc=1, device_id=partner, device_id_type=MESH)
    pl.semaphore_wait(barrier, len(partners))


def scale_rows(ref, rows, columns, factor, step=32):
    def body(i, carry):
        at = pl.ds(mult(i * step, step), step)
        wide = ref[at, :].astype(jnp.float32)
        ref[at, :] = jnp.floor(wide * factor + 0.5).astype(jnp.bfloat16)
        return carry

    lax.fori_loop(0, rows // step, body, 0)


def kernel_in(widths, bases, tokens, gate, up, down, *refs):
    refs = list(refs)

    def take(n):
        out = refs[:n]
        del refs[:n]
        return out

    hidden_out = take(3)
    (peaks_out,) = take(1)
    down_land = take(3)
    gate_w, up_w, tok, part, near, total, far = (take(3) for _ in range(7))
    acc, peak_send, peak_recv, send_sems, recv_sems, own_sems, load_sems = take(7)
    toks, feat = tokens.shape
    quarter, slab = toks // 4, toks // 16
    xyz, core = place()
    other = 1 - core

    partners = [device_at(xyz, other)]
    for axis in range(3):
        for step in range(1, SIDE):
            for c in range(2):
                partners.append(device_at(moved(xyz, axis, step), c))
    greet(partners)

    mail = Mail(send_sems, recv_sems)
    own = []

    def spread(kind):
        arrivals = [[], [], []]
        for step in range(SIDE):
            for flip in range(2):
                if step == 0 and flip == 0:
                    continue
                for g in range(3):
                    there = moved(xyz, g, step)
                    peer_core = core if flip == 0 else other
                    slot = mult((xyz[g] * 2 + core) * feat, feat)
                    part_no = there[g] * 2 + peer_core
                    if kind == 2:
                        src, dst = tokens, tok[g].at[:, pl.ds(slot, feat)]
                    else:
                        col = mult(bases[g] + part_no * widths[g], 128)
                        src = (gate, up)[kind].at[:, pl.ds(col, widths[g])]
                        dst = (gate_w, up_w)[kind][g].at[pl.ds(slot, feat), :]
                    arrivals[g].append(mail.post(src, dst, device_at(there, peer_core)))
        for g in range(3):
            slot = mult((xyz[g] * 2 + core) * feat, feat)
            if kind == 2:
                src, dst = tokens, tok[g].at[:, pl.ds(slot, feat)]
            else:
                col = mult(bases[g] + (xyz[g] * 2 + core) * widths[g], 128)
                src = (gate, up)[kind].at[:, pl.ds(col, widths[g])]
                dst = (gate_w, up_w)[kind][g].at[pl.ds(slot, feat), :]
            copy = pltpu.make_async_copy(src, dst, own_sems.at[kind * 3 + g])
            copy.start()
            own.append(copy)
        return arrivals

    gate_in = spread(0)
    tok_in = spread(2)
    up_in = spread(1)

    def peak_of(load, wave):
        slots = load(wave)
        best = None
        for view in slots:
            rows, cols = view.shape

            def body(i, carry, view=view):
                return jnp.maximum(carry, jnp.abs(view[pl.ds(mult(i * 16, 16), 16), :]))

            top = lax.fori_loop(0, rows // 16, body, jnp.zeros((16, cols), jnp.bfloat16))
            top = jnp.max(top.astype(jnp.float32))
            best = top if best is None else jnp.maximum(best, top)
        return best

    def load_rows(source):
        def run(wave):
            views, copies = [], []
            total_cols = source.shape[1]
            at = 0
            for g in range(3):
                for k in range(2):
                    for r in range(toks // feat):
                        width = min(widths[g], total_cols - at)
                        if width <= 0:
                            continue
                        view = part[g].at[k, pl.ds(r * feat, feat), pl.ds(0, width)]
                        copies.append(
                            pltpu.make_async_copy(
                                source.at[:, pl.ds(at, width)], view, load_sems.at[len(views)]
                            )
                        )
                        views.append(view)
                        at += width
            for copy in copies:
                copy.start()
            for copy in copies:
                copy.wait()
            return views

        return run

    def load_columns(source):
        def run(wave):
            views, copies = [], []
            total_rows = source.shape[0]
            at = 0
            for g in range(3):
                for k in range(2):
                    for j in range(widths[g] // feat):
                        height = min(toks, total_rows - at)
                        if height <= 0:
                            continue
                        view = part[g].at[k, pl.ds(0, height), pl.ds(j * feat, feat)]
                        copies.append(
                            pltpu.make_async_copy(
                                source.at[pl.ds(at, height), :], view, load_sems.at[len(views)]
                            )
                        )
                        views.append(view)
                        at += height
            for copy in copies:
                copy.start()
            for copy in copies:
                copy.wait()
            return views

        return run

    tops = [
        peak_of(load_rows(gate), 0),
        peak_of(load_rows(up), 1),
        peak_of(load_columns(down), 2),
    ]
    row = lax.broadcasted_iota(jnp.int32, (8, 128), 0)
    tile = jnp.where(row == 0, tops[0], jnp.where(row == 1, tops[1], tops[2]))
    got = 0
    for axis in range(3):
        peak_send[axis] = tile
        waits = []
        for step in range(SIDE):
            for flip in range(2):
                if step == 0 and flip == 0 or axis > 0 and flip == 1:
                    continue
                there = device_at(moved(xyz, axis, step), core if flip == 0 else other)
                waits.append(mail.post(peak_send.at[axis], peak_recv.at[got], there))
                got += 1
        for back, copy in enumerate(waits):
            copy.wait_recv()
            tile = jnp.maximum(tile, peak_recv[got - len(waits) + back])
    peaks_out[...] = tile
    peaks = [jnp.max(tile[k : k + 1, :]) for k in range(3)]
    factors = [jnp.max(127.0 / tile[k : k + 1, :]) for k in range(3)]
    units = [jnp.max(tile[k : k + 1, :] / 127.0) for k in range(3)]

    def partial_sums(kind, g, weights):
        width = widths[g]
        cols = 384 if width % 384 == 0 else 256 if width % 256 == 0 else 128
        b = xyz[SUM_AXES[g][0]]

        def body(j, carry):
            at = pl.ds(mult(j * cols, 128), cols)
            acc[:, pl.ds(0, cols)] = jnp.dot(
                tok[g][...], weights[:, at], preferred_element_type=jnp.float32
            )
            part[g][kind, :, at] = acc[:, pl.ds(0, cols)].astype(jnp.bfloat16)
            mine = pl.ds(mult(b * quarter, quarter), quarter)
            total[g][kind, :, at] = acc[mine, pl.ds(0, cols)]
            return carry

        lax.fori_loop(0, width // cols, body, 0)

    near_in = [[], [], []]

    def send_near(kind, g):
        axis = SUM_AXES[g][0]
        for step in (2, 1, 3):
            there = moved(xyz, axis, step)
            rows = pl.ds(mult(there[axis] * quarter, quarter), quarter)
            near_in[g].append(
                mail.post(
                    part[g].at[kind, rows, :],
                    near[g].at[kind, step - 1],
                    device_at(there, core),
                )
            )

    down_in = []

    def spread_down():
        for step in (2, 1, 3):
            for g in range(3):
                there = moved(xyz, g, step)
                start = mult(bases[g] + there[g] * 2 * widths[g], 128)
                down_in.append(
                    mail.post(
                        down.at[pl.ds(start, 2 * widths[g]), :],
                        down_land[g].at[:, pl.ds(mult(xyz[g] * feat, feat), feat)],
                        device_at(there, core),
                    )
                )
        for g in range(3):
            start = mult(bases[g] + xyz[g] * 2 * widths[g], 128)
            copy = pltpu.make_async_copy(
                down.at[pl.ds(start, 2 * widths[g]), :],
                down_land[g].at[:, pl.ds(mult(xyz[g] * feat, feat), feat)],
                own_sems.at[9 + g],
            )
            copy.start()
            own.append(copy)

    for kind, (weights, arrivals) in enumerate(((gate_w, gate_in), (up_w, up_in))):
        for g in range(3):
            for copy in arrivals[g]:
                copy.wait_recv()
            own[kind * 6 + g].wait()
            scale_rows(weights[g], 8 * feat, widths[g], factors[kind])
            if kind == 0:
                for copy in tok_in[g]:
                    copy.wait_recv()
                own[3 + g].wait()
            partial_sums(kind, g, weights[g])
            send_near(kind, g)
            if kind == 1 and g == 0:
                spread_down()

    far_in = [[], [], []]
    for g in range(3):
        axis = SUM_AXES[g][1]
        for copy in near_in[g]:
            copy.wait_recv()
        for kind in range(2):

            def body(i, carry, kind=kind, g=g):
                at = pl.ds(mult(i * 16, 16), 16)
                terms = [near[g][kind, n, at, :].astype(jnp.float32) for n in range(3)]
                total[g][kind, at, :] = (total[g][kind, at, :] + terms[1]) + (terms[0] + terms[2])
                return carry

            lax.fori_loop(0, quarter // 16, body, 0)
            for step in (2, 1, 3):
                there = moved(xyz, axis, step)
                rows = pl.ds(mult(there[axis] * slab, slab), slab)
                far_in[g].append(
                    mail.post(
                        total[g].at[kind, rows, :],
                        far[g].at[kind, step - 1],
                        device_at(there, core),
                    )
                )
    for g in range(3):
        axis = SUM_AXES[g][1]
        for copy in far_in[g]:
            copy.wait_recv()

        def body(i, carry, g=g, axis=axis):
            at = pl.ds(mult(i * 16, 16), 16)
            mine = pl.ds(mult(xyz[axis] * slab + i * 16, 16), 16)
            sums = []
            for kind in range(2):
                value = (total[g][kind, mine, :] + far[g][kind, 1, at, :]) + (
                    far[g][kind, 0, at, :] + far[g][kind, 2, at, :]
                )
                sums.append(value * units[kind])
            hidden = sums[0] / (1.0 + jnp.exp(-sums[0])) * sums[1]
            hidden_out[g][at, :] = hidden.astype(jnp.bfloat16)
            return carry

        lax.fori_loop(0, slab // 16, body, 0)
    for copy in down_in:
        copy.wait_recv()
    for copy in own[9:]:
        copy.wait()
    mail.finish()


def kernel_out(widths, *refs):
    refs = list(refs)

    def take(n):
        out = refs[:n]
        del refs[:n]
        return out

    hidden_in = take(3)
    (peaks,) = take(1)
    down_land = take(3)
    (out,) = take(1)
    hidden, down_w, sent, landed = (take(3) for _ in range(4))
    acc, total, send_sems, recv_sems, own_sems = take(5)
    toks, feat = out.shape
    quarter, slab = toks // 4, toks // 16
    xyz, core = place()
    other = 1 - core

    partners = [device_at(xyz, other)]
    for axis in range(3):
        for step in range(1, SIDE):
            partners.append(device_at(moved(xyz, axis, step), core))
    greet(partners)

    mail = Mail(send_sems, recv_sems)
    slab_in, own = [[], [], []], []
    for g in range(3):
        b_axis, c_axis = SUM_AXES[g]
        row = mult(xyz[b_axis] * quarter + xyz[c_axis] * slab, slab)
        home = hidden[g].at[core, pl.ds(row, slab), :]
        for step in (2, 1, 3):
            slab_in[g].append(
                mail.post(hidden_in[g], home, device_at(moved(xyz, c_axis, step), core))
            )
        copy = pltpu.make_async_copy(hidden_in[g], home, own_sems.at[g])
        copy.start()
        own.append(copy)
    for g in range(3):
        copy = pltpu.make_async_copy(down_land[g], down_w[g], own_sems.at[3 + g])
        copy.start()
        own.append(copy)
    factor = jnp.max(127.0 / peaks[2:3, :])
    unit = jnp.max(peaks[2:3, :] / 127.0)

    quarter_in, cross_in = [[], [], []], [[], [], []]

    def cross(g, step):
        b_axis = SUM_AXES[g][0]
        from_b = lax.rem(xyz[b_axis] + SIDE - step, SIDE)
        view = hidden[g].at[core, pl.ds(mult(from_b * quarter, quarter), quarter), :]
        cross_in[g].append(mail.post(view, view, device_at(xyz, other)))

    for g in range(3):
        b_axis = SUM_AXES[g][0]
        for copy in slab_in[g]:
            copy.wait_recv()
        own[g].wait()
        view = hidden[g].at[core, pl.ds(mult(xyz[b_axis] * quarter, quarter), quarter), :]
        for step in (2, 1, 3):
            quarter_in[g].append(
                mail.post(view, view, device_at(moved(xyz, b_axis, step), core))
            )
        cross(g, 0)
    for g in range(3):
        own[3 + g].wait()
        scale_rows(down_w[g], 2 * widths[g], 4 * feat, factor)
    landed_in = [[], [], []]
    for g in range(3):
        for copy, step in zip(quarter_in[g], (2, 1, 3)):
            copy.wait_recv()
            cross(g, step)
    for g in range(3):
        for copy in cross_in[g]:
            copy.wait_recv()
        width = widths[g]

        def body(i, carry, g=g, width=width):
            rows = pl.ds(mult(i * quarter, quarter), quarter)
            value = jnp.dot(
                hidden[g][0, rows, :], down_w[g][pl.ds(0, width), :],
                preferred_element_type=jnp.float32,
            ) + jnp.dot(
                hidden[g][1, rows, :], down_w[g][pl.ds(width, width), :],
                preferred_element_type=jnp.float32,
            )
            for j in range(SIDE):
                block = value[:, j * feat : (j + 1) * feat]
                acc[j, rows, :] = block
                sent[g][j, rows, :] = block.astype(jnp.bfloat16)
            mine = acc[xyz[g], rows, :]
            if g == 0:
                total[rows, :] = mine
            else:
                total[rows, :] = total[rows, :] + mine
            return carry

        lax.fori_loop(0, SIDE, body, 0)
        for step in (2, 1, 3):
            there = moved(xyz, g, step)
            landed_in[g].append(
                mail.post(sent[g].at[there[g]], landed[g].at[step - 1], device_at(there, core))
            )
    for g in range(3):
        for copy in landed_in[g]:
            copy.wait_recv()
    value = total[...]
    for g in range(3):
        for n in range(3):
            value = value + landed[g][n].astype(jnp.float32)
    out[...] = (value * unit).astype(jnp.bfloat16)
    mail.finish()


def shards(tokens, gate_weight, up_weight, down_weight):
    toks, feat = tokens.shape
    ff = gate_weight.shape[1]
    widths = class_widths(ff)
    bases = class_bases(widths)
    quarter, slab = toks // 4, toks // 16
    bf16, f32 = jnp.bfloat16, jnp.float32
    hbm = pl.BlockSpec(memory_space=pl.ANY)
    vmem = pl.BlockSpec(memory_space=pltpu.VMEM)
    shape = jax.ShapeDtypeStruct

    scratch = [pltpu.VMEM((8 * feat, w), bf16) for w in widths] * 2
    scratch += [pltpu.VMEM((toks, 8 * feat), bf16) for _ in widths]
    scratch += [pltpu.VMEM((2, toks, w), bf16) for w in widths]
    scratch += [pltpu.VMEM((2, 3, quarter, w), bf16) for w in widths]
    scratch += [pltpu.VMEM((2, quarter, w), f32) for w in widths]
    scratch += [pltpu.VMEM((2, 3, slab, w), f32) for w in widths]
    scratch += [
        pltpu.VMEM((toks, 384), f32),
        pltpu.VMEM((3, 8, 128), f32),
        pltpu.VMEM((13, 8, 128), f32),
        pltpu.SemaphoreType.DMA((121,)),
        pltpu.SemaphoreType.DMA((121,)),
        pltpu.SemaphoreType.DMA((12,)),
        pltpu.SemaphoreType.DMA((36,)),
    ]
    outs = pl.pallas_call(
        functools.partial(kernel_in, widths, bases),
        out_shape=(
            *[shape((slab, w), bf16) for w in widths],
            shape((8, 128), f32),
            *[shape((2 * w, 4 * feat), bf16) for w in widths],
        ),
        in_specs=[hbm] * 4,
        out_specs=(vmem, vmem, vmem, vmem, hbm, hbm, hbm),
        scratch_shapes=scratch,
        compiler_params=pltpu.CompilerParams(
            collective_id=0, has_side_effects=True, vmem_limit_bytes=60 * 2**20
        ),
        name="refit_in",
    )(tokens, gate_weight, up_weight, down_weight)
    hidden, peaks, down_land = outs[:3], outs[3], outs[4:]

    scratch = [pltpu.VMEM((2, toks, w), bf16) for w in widths]
    scratch += [pltpu.VMEM((2 * w, 4 * feat), bf16) for w in widths]
    scratch += [pltpu.VMEM((SIDE, toks, feat), bf16) for w in widths]
    scratch += [pltpu.VMEM((3, toks, feat), bf16) for w in widths]
    scratch += [
        pltpu.VMEM((SIDE, toks, feat), f32),
        pltpu.VMEM((toks, feat), f32),
        pltpu.SemaphoreType.DMA((39,)),
        pltpu.SemaphoreType.DMA((39,)),
        pltpu.SemaphoreType.DMA((6,)),
    ]
    output_block = pl.pallas_call(
        functools.partial(kernel_out, widths),
        out_shape=shape((toks, feat), bf16),
        in_specs=[vmem] * 4 + [hbm] * 3,
        out_specs=vmem,
        scratch_shapes=scratch,
        compiler_params=pltpu.CompilerParams(
            collective_id=1, has_side_effects=True, vmem_limit_bytes=60 * 2**20
        ),
        name="refit_out",
    )(*hidden, peaks, *down_land)
    return output_block, peaks[:3, 0]


def solution(mesh):
    in_specs = (
        P(None, ("rep", "tp")),
        P(("rep", "tp"), None),
        P(("rep", "tp"), None),
        P(None, ("rep", "tp")),
    )
    out_specs = (P(None, ("rep", "tp")), P())
    return jax.shard_map(shards, mesh=mesh, in_specs=in_specs, out_specs=out_specs, check_vma=False)
```

time: 669 us -> 238 us (0.36)
  waiting for transfers between devices: 359 us -> 0 us
  Pallas kernels: 0 us -> 235 us
  blocking collectives: 155 us -> 0 us
  local copies, waits for them, and re-layouts: 50.3 us -> 2.25 us
  other arithmetic: 38.6 us -> 0 us
  matrix products: 32.7 us -> 0 us
  between operations: 17.8 us -> 0.66 us
  starting transfers between devices: 13.5 us -> 0 us
    pallas_call x0 -> x2, Pallas kernels: none -> 235 us  [the longest x1 182 us: shards(): pl.pallas_call(functools.partial(kernel_in, widths, bases), out_shape=(*[...]
    all_to_all x2 -> x0, waiting for transfers between devices: 178 us -> none  [the longest x1 104 us: shards(): lax.all_to_all(gate_weight, 'rep', split_axis=1, concat_axis=0, tiled=True)]
    psum x1 -> x0, waiting for transfers between devices: 98.8 us -> none  [shards(): gate_sum, up_sum = lax.psum((gate_part, up_part), 'tp')]
    all_to_all x1 -> x0, blocking collectives: 83.7 us -> none  [shards(): lax.all_to_all(up_weight, 'rep', split_axis=1, concat_axis=0, tiled=True)]
    reduce_scatter x1 -> x0, waiting for transfers between devices: 80.7 us -> none  [shards(): lax.psum_scatter(partial_out, 'rep', scatter_dimension=1, tiled=True)]
    pmax x1 -> x0, blocking collectives: 71.4 us -> none  [shards(): lax.pmax(local_peaks(gate_cols, up_cols, down_rows), ('rep', 'tp'))]
    dot_general x3 -> x0, matrix products: 32.7 us -> none  [the longest x1 12.9 us: shards(): jnp.dot(hidden, scaled_copy(down_rows, peak_values[2]), preferred_element...]
    another operation x3 -> x0, local copies, waits for them, and re-layouts: 29.5 us -> none
  transfers between devices with their start and end apart: 5 -> 0, of which waited for: 4 -> 0; matrix products, arithmetic and copies ran while one was open for 12% -> 0% of each run, Pallas kernels for 0% -> 0%
where the time goes in v1:
time: 238 us; the launch traced here: 237 us
  Pallas kernels  235 us (99%)
    pallas_call x1, Pallas kernels, shards(): pl.pallas_call(functools.partial(kernel_in, widths, bases), out_shape=(*[...  182 us
    pallas_call x1, Pallas kernels, shards(): pl.pallas_call(functools.partial(kernel_out, widths), out_shape=shape((to...  52.7 us

profile of v1, /device:TPU:1, one launch (start us, length us, event | category | flops | bytes accessed | tf_op | source)
XLA Modules:
  0.0 237.4 jit_solution(5313872803693725773)
XLA Ops:
  0.6 181.8 %refit_in.1 = (bf16[48,1152]{1,0:T(8,128)(2,1)}, bf16[48,1152]{1,0:T(8,128)(2,1)}, bf16[48,1024]{1,0:T(8,128)(2,1)}, f32[8,128]{1,0:T(8,128)}, bf16[2304,512]{1,...) custom-call(bf16[768,128]{1,0:T(8,128)(2,1)} %tokens.1, bf16[128,26624]{1,0:T(8,128)(2,1)} %gate.1, ...), custom_call_target="tpu_custom_call" | custom-call | tf_op jit(solution)/shard_map/refit_in/pallas_call | solution.py:504
  182.5 0.0 copy-start
  182.5 52.7 %refit_out.1 = bf16[768,128]{1,0:T(8,128)(2,1)} custom-call(bf16[48,1152]{1,0:T(8,128)(2,1)} %get-tuple-element.9.refs_0_, bf16[48,1152]{1,0:T(8,128)(2,1)} %get-tuple-element.10.refs_1_, bf16[48,1024]{1,0:T(8,128)(2,1)} %get-tuple-element.11.refs_2_, f32[8,128]{1,0:T(8,128)} %get-tuple-element.12.refs_3_, bf16[2304,512]{1,0:T(8,128)(2,1)} %get-tuple-element.13.refs_4_, ...), custom_call_target="tpu_custom_call" | custom-call | tf_op jit(solution)/shard_map/refit_out/pallas_call | solution.py:532
  235.2 0.0 copy-done
  235.2 0.6 slice_reduce_fusion
  235.8 1.6 copy.7
Async XLA Ops:
  182.5 52.7 %copy-start = (f32[8,128]{1,0:T(8,128)S(1)}, f32[8,128]{1,0:T(8,128)}, u32[]{:S(2)}) copy-start(f32[8,128]{1,0:T(8,128)} %get-tuple-element.12.refs_3_) | copy-start | bytes 12292

commit v2 on v0

v2 whole, which is shorter than its diff:
```python
import functools

import jax
import jax.numpy as jnp
from jax import lax
from jax.experimental import pallas as pl
from jax.experimental.pallas import tpu as pltpu
from jax.sharding import PartitionSpec as P

MESH = pl.DeviceIdType.MESH
SIDE = 4
SUM_AXES = ((1, 2), (2, 0), (0, 1))


def class_widths(ff):
    units = ff // (8 * 128)
    first = (units + 2) // 3
    second = (units - first + 1) // 2
    return [first * 128, second * 128, (units - first - second) * 128]


def class_bases(widths):
    return [0, 8 * widths[0], 8 * (widths[0] + widths[1])]


def place():
    rep = lax.axis_index("rep")
    tp = lax.axis_index("tp")
    return (rep // SIDE, tp // 2, lax.rem(rep, SIDE)), lax.rem(tp, 2)


def device_at(xyz, core):
    return (xyz[0] * SIDE + xyz[2], xyz[1] * 2 + core)


def moved(xyz, axis, step):
    out = list(xyz)
    out[axis] = lax.rem(xyz[axis] + step, SIDE)
    return tuple(out)


def mult(value, of):
    return pl.multiple_of(value, of)


class Mail:
    def __init__(self, send_sems, recv_sems):
        self.send_sems, self.recv_sems, self.used, self.sent = send_sems, recv_sems, 0, []

    def post(self, src, dst, device):
        copy = pltpu.make_async_remote_copy(
            src_ref=src,
            dst_ref=dst,
            send_sem=self.send_sems.at[self.used],
            recv_sem=self.recv_sems.at[self.used],
            device_id=device,
            device_id_type=MESH,
        )
        self.used += 1
        copy.start()
        self.sent.append(copy)
        return copy

    def finish(self):
        for copy in self.sent:
            copy.wait_send()


def greet(partners):
    barrier = pltpu.get_barrier_semaphore()
    for partner in partners:
        pl.semaphore_signal(barrier, inc=1, device_id=partner, device_id_type=MESH)
    pl.semaphore_wait(barrier, len(partners))


def scale_rows(ref, rows, columns, factor, step=32):
    def body(i, carry):
        at = pl.ds(mult(i * step, step), step)
        wide = ref[at, :].astype(jnp.float32)
        ref[at, :] = jnp.floor(wide * factor + 0.5).astype(jnp.bfloat16)
        return carry

    lax.fori_loop(0, rows // step, body, 0)


def kernel(widths, bases, tokens, gate, up, down, *refs):
    refs = list(refs)

    def take(n):
        out = refs[:n]
        del refs[:n]
        return out

    out, peaks_out = take(2)
    down_land = take(3)
    gate_w, up_w, tok, part, near, half, total, far, hidden, sent, landed = (
        take(3) for _ in range(11)
    )
    acc, blocks, mine_out, peak_send, peak_recv = take(5)
    send_sems, recv_sems, own_sems, load_sems = take(4)
    toks, feat = tokens.shape
    quarter, slab = toks // 4, toks // 16
    mid = quarter // 2
    xyz, core = place()
    other = 1 - core
    mail = Mail(send_sems, recv_sems)

    def load(source, spots, first):
        copies = []
        for g in range(3):
            if source is down:
                pieces = 2 * (widths[g] // feat)
            else:
                pieces = 8
            for p in range(pieces):
                if source is down:
                    rows = 4 * feat
                    start = bases[g] + p * rows
                    view = spots[g].at[
                        p % 2, pl.ds(0, rows), pl.ds((p // 2) * feat, feat)
                    ]
                    origin = source.at[pl.ds(start, rows), :]
                else:
                    view = spots[g].at[p // 4, pl.ds((p % 4) * feat, feat), :]
                    origin = source.at[:, pl.ds(bases[g] + p * widths[g], widths[g])]
                copies.append(
                    pltpu.make_async_copy(origin, view, load_sems.at[first + len(copies)])
                )
        for copy in copies:
            copy.start()
        return copies

    def top_of(spots, copies):
        for copy in copies:
            copy.wait()
        best = None
        for g in range(3):

            def body(i, carry, g=g):
                at = pl.ds(mult(i * 32, 32), 32)
                return jnp.maximum(
                    carry, jnp.maximum(jnp.abs(spots[g][0, at, :]), jnp.abs(spots[g][1, at, :]))
                )

            high = lax.fori_loop(
                0, 4 * feat // 32, body, jnp.zeros((32, widths[g]), jnp.bfloat16)
            )
            high = jnp.max(high.astype(jnp.float32))
            best = high if best is None else jnp.maximum(best, high)
        return best

    gate_load = load(gate, part, 0)
    up_load = load(up, hidden, 24)

    own = {}

    def keep(name, src, dst, sem):
        copy = pltpu.make_async_copy(src, dst, own_sems.at[sem])
        copy.start()
        own[name] = copy

    def token_spot(g, position, c):
        return tok[g].at[:, pl.ds(mult((position * 2 + c) * feat, feat), feat)]

    def weight_spot(kind, g):
        slot = mult((xyz[g] * 2 + core) * feat, feat)
        return (gate_w, up_w)[kind][g].at[pl.ds(slot, feat), pl.ds(0, widths[g])]

    def weight_part(kind, g, position, c):
        col = mult(bases[g] + (position * 2 + c) * widths[g], 128)
        return (gate, up)[kind].at[:, pl.ds(col, widths[g])]

    for g in range(3):
        keep(("tok", g), tokens, token_spot(g, xyz[g], core), g)
        for kind in range(2):
            keep((kind, g), weight_part(kind, g, xyz[g], core), weight_spot(kind, g), 3 + 2 * g + kind)

    partners = [device_at(xyz, other)]
    for axis in range(3):
        for step in range(1, SIDE):
            for c in range(2):
                partners.append(device_at(moved(xyz, axis, step), c))
    greet(partners)

    tok_in, tok_cross = [[], [], []], [[], [], []]
    for step in (2, 1, 3):
        for g in range(3):
            tok_in[g].append(
                (
                    step,
                    mail.post(
                        tokens, token_spot(g, xyz[g], core), device_at(moved(xyz, g, step), core)
                    ),
                )
            )
    for g in range(3):
        tok_cross[g].append(
            mail.post(tokens, token_spot(g, xyz[g], core), device_at(xyz, other))
        )

    weight_in = {}

    def send_weights(kind, step, flip):
        for g in range(3):
            there = moved(xyz, g, step)
            c = core if flip == 0 else other
            weight_in.setdefault((kind, g), []).append(
                mail.post(
                    weight_part(kind, g, there[g], c), weight_spot(kind, g), device_at(there, c)
                )
            )

    gate_top = top_of(part, gate_load)
    down_load = load(down, part, 48)
    up_top = top_of(hidden, up_load)
    down_top = top_of(part, down_load)
    row = lax.broadcasted_iota(jnp.int32, (8, 128), 0)
    tile = jnp.where(row == 0, gate_top, jnp.where(row == 1, up_top, down_top))

    got = 0
    for axis in range(3):
        peak_send[axis] = tile
        waits = []
        for step in range(SIDE):
            for flip in range(2):
                if step == 0 and flip == 0 or axis > 0 and flip == 1:
                    continue
                there = device_at(moved(xyz, axis, step), core if flip == 0 else other)
                waits.append((got, mail.post(peak_send.at[axis], peak_recv.at[got], there)))
                got += 1
        if axis < 2:
            send_weights(0, 1, axis)
            send_weights(0, 3, axis)
        else:
            send_weights(0, 2, 0)
            send_weights(0, 2, 1)
            send_weights(0, 0, 1)
            for flip in range(2):
                for step in (2, 1, 3):
                    send_weights(1, step, flip)
            send_weights(1, 0, 1)
        if axis == 1:
            for g in range(3):
                for step, copy in tok_in[g]:
                    copy.wait_recv()
                    spot = token_spot(g, lax.rem(xyz[g] + SIDE - step, SIDE), core)
                    tok_cross[g].append(mail.post(spot, spot, device_at(xyz, other)))
        for n, copy in waits:
            copy.wait_recv()
            tile = jnp.maximum(tile, peak_recv[n])
    peaks_out[...] = tile
    factors = [jnp.max(127.0 / tile[k : k + 1, :]) for k in range(3)]
    units = [jnp.max(tile[k : k + 1, :] / 127.0) for k in range(3)]

    def partial_sums(kind, g):
        width = widths[g]
        cols = 384 if width % 384 == 0 else 256 if width % 256 == 0 else 128
        b = xyz[SUM_AXES[g][0]]
        weights = (gate_w, up_w)[kind][g]

        def body(j, carry):
            at = pl.ds(mult(j * cols, 128), cols)
            acc[:, pl.ds(0, cols)] = jnp.dot(
                tok[g][...], weights[pl.ds(0, 8 * feat), at], preferred_element_type=jnp.float32
            )
            part[g][kind, :, at] = acc[:, pl.ds(0, cols)].astype(jnp.bfloat16)
            mine = pl.ds(mult(b * quarter, quarter), quarter)
            total[g][kind, :, at] = acc[mine, pl.ds(0, cols)]
            return carry

        lax.fori_loop(0, width // cols, body, 0)

    near_in, half_in = {}, {}

    def rows_of(position, first, count):
        return pl.ds(mult(position * quarter + first, 16), count)

    def send_near(kind, g):
        axis = SUM_AXES[g][0]
        after, before, far_off = (moved(xyz, axis, s) for s in (1, 3, 2))
        half_in[kind, g] = [
            mail.post(
                part[g].at[kind, rows_of(far_off[axis], 0, mid), :],
                half[g].at[kind, 0],
                device_at(after, core),
            ),
            mail.post(
                part[g].at[kind, rows_of(far_off[axis], mid, mid), :],
                half[g].at[kind, 1],
                device_at(before, core),
            ),
        ]
        near_in[kind, g] = [
            mail.post(
                part[g].at[kind, rows_of(after[axis], mid, mid), :],
                near[g].at[kind, 0, pl.ds(mid, mid), :],
                device_at(after, core),
            ),
            mail.post(
                part[g].at[kind, rows_of(before[axis], 0, mid), :],
                near[g].at[kind, 1, pl.ds(0, mid), :],
                device_at(before, core),
            ),
        ]

    def pass_near(kind, g):
        axis = SUM_AXES[g][0]
        for n, (step, first) in enumerate(((1, 0), (3, mid))):
            there = moved(xyz, axis, step)
            half_in[kind, g][n].wait_recv()

            def body(i, carry, n=n, first=first, there=there):
                at = rows_of(there[axis], first + i * 16, 16)
                value = part[g][kind, at, :].astype(jnp.float32) + half[g][
                    kind, n, pl.ds(mult(i * 16, 16), 16), :
                ].astype(jnp.float32)
                part[g][kind, at, :] = value.astype(jnp.bfloat16)
                return carry

            lax.fori_loop(0, mid // 16, body, 0)
            near_in[kind, g].append(
                mail.post(
                    part[g].at[kind, rows_of(there[axis], first, mid), :],
                    near[g].at[kind, n, pl.ds(first, mid), :],
                    device_at(there, core),
                )
            )

    down_in = [[], [], []]

    def send_down(step):
        for g in range(3):
            there = moved(xyz, g, step)
            start = mult(bases[g] + there[g] * 2 * widths[g], 128)
            src = down.at[pl.ds(start, 2 * widths[g]), :]
            dst = down_land[g].at[:, pl.ds(mult(xyz[g] * feat, feat), feat)]
            if step == 0:
                keep(("down", g), src, dst, 9 + g)
            else:
                down_in[g].append(mail.post(src, dst, device_at(there, core)))

    for kind in range(2):
        for g in range(3):
            for copy in weight_in[kind, g]:
                copy.wait_recv()
            own[kind, g].wait()
            scale_rows((gate_w, up_w)[kind][g], 8 * feat, widths[g], factors[kind])
            if kind == 0:
                for copy in tok_cross[g]:
                    copy.wait_recv()
                own["tok", g].wait()
            partial_sums(kind, g)
            send_near(kind, g)
    send_down(0)
    for kind in range(2):
        for g in range(3):
            pass_near(kind, g)
    send_down(1)
    send_down(3)

    far_in = [[], [], []]
    for kind in range(2):
        for g in range(3):
            axis = SUM_AXES[g][1]
            for copy in near_in[kind, g]:
                copy.wait_recv()

            def body(i, carry, kind=kind, g=g):
                at = pl.ds(mult(i * 16, 16), 16)
                total[g][kind, at, :] = total[g][kind, at, :] + (
                    near[g][kind, 0, at, :].astype(jnp.float32)
                    + near[g][kind, 1, at, :].astype(jnp.float32)
                )
                return carry

            lax.fori_loop(0, quarter // 16, body, 0)
            for step in (2, 1, 3):
                there = moved(xyz, axis, step)
                rows = pl.ds(mult(there[axis] * slab, slab), slab)
                far_in[g].append(
                    mail.post(
                        total[g].at[kind, rows, :],
                        far[g].at[kind, step - 1],
                        device_at(there, core),
                    )
                )
    send_down(2)

    slab_in = [[], [], []]
    for g in range(3):
        b_axis, c_axis = SUM_AXES[g]
        for copy in far_in[g]:
            copy.wait_recv()
        start = xyz[b_axis] * quarter + xyz[c_axis] * slab

        def body(i, carry, g=g, c_axis=c_axis, start=start):
            at = pl.ds(mult(i * 16, 16), 16)
            mine = pl.ds(mult(xyz[c_axis] * slab + i * 16, 16), 16)
            sums = []
            for kind in range(2):
                value = (total[g][kind, mine, :] + far[g][kind, 1, at, :]) + (
                    far[g][kind, 0, at, :] + far[g][kind, 2, at, :]
                )
                sums.append(value * units[kind])
            value = sums[0] / (1.0 + jnp.exp(-sums[0])) * sums[1]
            hidden[g][core, pl.ds(mult(start + i * 16, 16), 16), :] = value.astype(jnp.bfloat16)
            return carry

        lax.fori_loop(0, slab // 16, body, 0)
        home = hidden[g].at[core, pl.ds(mult(start, slab), slab), :]
        for step in (2, 1, 3):
            slab_in[g].append(mail.post(home, home, device_at(moved(xyz, c_axis, step), core)))

    quarter_in, rest_in, cross_in = [[], [], []], [[], [], []], [[], [], []]

    def hidden_rows(g, step, first, count):
        position = lax.rem(xyz[SUM_AXES[g][0]] + step, SIDE)
        return hidden[g].at[core, rows_of(position, first, count), :]

    def cross(g, step):
        view = hidden_rows(g, step, 0, quarter)
        cross_in[g].append(mail.post(view, view, device_at(xyz, other)))

    for g in range(3):
        axis = SUM_AXES[g][0]
        for copy in slab_in[g]:
            copy.wait_recv()
        view = hidden_rows(g, 0, 0, quarter)
        for step in (1, 3):
            quarter_in[g].append(mail.post(view, view, device_at(moved(xyz, axis, step), core)))
        cross(g, 0)

    for g in range(3):
        for copy in down_in[g]:
            copy.wait_recv()
        own["down", g].wait()
        for p in range(2):
            keep(
                ("down", g, p),
                down_land[g].at[pl.ds(p * widths[g], widths[g]), :],
                gate_w[g].at[pl.ds(0, widths[g]), pl.ds(p * 4 * feat, 4 * feat)],
                12 + 2 * g + p,
            )
    mine_out[...] = jnp.zeros_like(mine_out)
    for g in range(3):
        for p in range(2):
            own["down", g, p].wait()
        scale_rows(gate_w[g], widths[g], 8 * feat, factors[2])

    for g in range(3):
        axis = SUM_AXES[g][0]
        quarter_in[g][0].wait_recv()
        view = hidden_rows(g, 3, 0, mid)
        rest_in[g].append(mail.post(view, view, device_at(moved(xyz, axis, 1), core)))
        quarter_in[g][1].wait_recv()
        view = hidden_rows(g, 1, mid, mid)
        rest_in[g].append(mail.post(view, view, device_at(moved(xyz, axis, 3), core)))
        cross(g, 3)
        cross(g, 1)

    landed_in = []

    def output_rows(g, n, step):
        cross_in[g][n].wait_recv()
        width = widths[g]
        rows = rows_of(lax.rem(xyz[SUM_AXES[g][0]] + step, SIDE), 0, quarter)
        value = jnp.dot(
            hidden[g][0, rows, :], gate_w[g][pl.ds(0, width), pl.ds(0, 4 * feat)],
            preferred_element_type=jnp.float32,
        ) + jnp.dot(
            hidden[g][1, rows, :], gate_w[g][pl.ds(0, width), pl.ds(4 * feat, 4 * feat)],
            preferred_element_type=jnp.float32,
        )
        for j in range(SIDE):
            block = value[:, j * feat : (j + 1) * feat]
            blocks[j] = block
            sent[g][j, rows, :] = block.astype(jnp.bfloat16)
        mine_out[rows, :] = mine_out[rows, :] + blocks[xyz[g]]
        for step in (2, 1, 3):
            there = moved(xyz, g, step)
            landed_in.append(
                mail.post(
                    sent[g].at[there[g], rows, :],
                    landed[g].at[step - 1, rows, :],
                    device_at(there, core),
                )
            )

    for n, step in ((0, 0), (1, 3), (2, 1)):
        for g in range(3):
            output_rows(g, n, step)
    for g in range(3):
        for copy in rest_in[g]:
            copy.wait_recv()
        cross(g, 2)
    for g in range(3):
        output_rows(g, 3, 2)
    for copy in landed_in:
        copy.wait_recv()
    value = mine_out[...]
    for g in range(3):
        for n in range(3):
            value = value + landed[g][n].astype(jnp.float32)
    out[...] = (value * units[2]).astype(jnp.bfloat16)
    mail.finish()


def shards(tokens, gate_weight, up_weight, down_weight):
    toks, feat = tokens.shape
    ff = gate_weight.shape[1]
    widths = class_widths(ff)
    bases = class_bases(widths)
    quarter, slab = toks // 4, toks // 16
    bf16, f32 = jnp.bfloat16, jnp.float32
    hbm = pl.BlockSpec(memory_space=pl.ANY)
    vmem = pl.BlockSpec(memory_space=pltpu.VMEM)
    shape = jax.ShapeDtypeStruct

    scratch = [pltpu.VMEM((max(8 * feat, w), max(8 * feat, w)), bf16) for w in widths]
    scratch += [pltpu.VMEM((8 * feat, w), bf16) for w in widths]
    scratch += [pltpu.VMEM((toks, 8 * feat), bf16) for _ in widths]
    scratch += [pltpu.VMEM((2, toks, w), bf16) for w in widths]
    scratch += [pltpu.VMEM((2, 2, quarter, w), bf16) for w in widths]
    scratch += [pltpu.VMEM((2, 2, quarter // 2, w), bf16) for w in widths]
    scratch += [pltpu.VMEM((2, quarter, w), f32) for w in widths]
    scratch += [pltpu.VMEM((2, 3, slab, w), f32) for w in widths]
    scratch += [pltpu.VMEM((2, toks, w), bf16) for w in widths]
    scratch += [pltpu.VMEM((SIDE, toks, feat), bf16) for _ in widths]
    scratch += [pltpu.VMEM((3, toks, feat), bf16) for _ in widths]
    scratch += [
        pltpu.VMEM((toks, 384), f32),
        pltpu.VMEM((SIDE, quarter, feat), f32),
        pltpu.VMEM((toks, feat), f32),
        pltpu.VMEM((3, 8, 128), f32),
        pltpu.VMEM((13, 8, 128), f32),
        pltpu.SemaphoreType.DMA((208,)),
        pltpu.SemaphoreType.DMA((208,)),
        pltpu.SemaphoreType.DMA((18,)),
        pltpu.SemaphoreType.DMA((100,)),
    ]
    outs = pl.pallas_call(
        functools.partial(kernel, widths, bases),
        out_shape=(
            shape((toks, feat), bf16),
            shape((8, 128), f32),
            *[shape((2 * w, 4 * feat), bf16) for w in widths],
        ),
        in_specs=[hbm] * 4,
        out_specs=(vmem, vmem, hbm, hbm, hbm),
        scratch_shapes=scratch,
        compiler_params=pltpu.CompilerParams(
            collective_id=0, has_side_effects=True, vmem_limit_bytes=63 * 2**20
        ),
        name="refit",
    )(tokens, gate_weight, up_weight, down_weight)
    return outs[0], outs[1][:3, 0]


def solution(mesh):
    in_specs = (
        P(None, ("rep", "tp")),
        P(("rep", "tp"), None),
        P(("rep", "tp"), None),
        P(None, ("rep", "tp")),
    )
    out_specs = (P(None, ("rep", "tp")), P())
    return jax.shard_map(shards, mesh=mesh, in_specs=in_specs, out_specs=out_specs, check_vma=False)
```

time: 669 us -> 190 us (0.28)
  waiting for transfers between devices: 359 us -> 0 us
  Pallas kernels: 0 us -> 186 us
  blocking collectives: 155 us -> 0 us
  local copies, waits for them, and re-layouts: 50.3 us -> 2.92 us
  other arithmetic: 38.6 us -> 0 us
  matrix products: 32.7 us -> 0 us
  between operations: 17.8 us -> 0.64 us
  starting transfers between devices: 13.5 us -> 0 us
    pallas_call x0 -> x1, Pallas kernels: none -> 186 us  [shards(): pl.pallas_call(functools.partial(kernel, widths, bases), out_shape=(shape...]
    all_to_all x2 -> x0, waiting for transfers between devices: 178 us -> none  [the longest x1 104 us: shards(): lax.all_to_all(gate_weight, 'rep', split_axis=1, concat_axis=0, tiled=True)]
    psum x1 -> x0, waiting for transfers between devices: 98.8 us -> none  [shards(): gate_sum, up_sum = lax.psum((gate_part, up_part), 'tp')]
    all_to_all x1 -> x0, blocking collectives: 83.7 us -> none  [shards(): lax.all_to_all(up_weight, 'rep', split_axis=1, concat_axis=0, tiled=True)]
    reduce_scatter x1 -> x0, waiting for transfers between devices: 80.7 us -> none  [shards(): lax.psum_scatter(partial_out, 'rep', scatter_dimension=1, tiled=True)]
    pmax x1 -> x0, blocking collectives: 71.4 us -> none  [shards(): lax.pmax(local_peaks(gate_cols, up_cols, down_rows), ('rep', 'tp'))]
    dot_general x3 -> x0, matrix products: 32.7 us -> none  [the longest x1 12.9 us: shards(): jnp.dot(hidden, scaled_copy(down_rows, peak_values[2]), preferred_element...]
    another operation x3 -> x0, local copies, waits for them, and re-layouts: 29.5 us -> none
  transfers between devices with their start and end apart: 5 -> 0, of which waited for: 4 -> 0; matrix products, arithmetic and copies ran while one was open for 12% -> 0% of each run, Pallas kernels for 0% -> 0%
where the time goes in v2:
time: 190 us
  Pallas kernels  186 us (98%)
  local copies, waits for them, and re-layouts  2.92 us (2%)
    pallas_call x1, Pallas kernels, shards(): pl.pallas_call(functools.partial(kernel, widths, bases), out_shape=(shape...  186 us

profile of v2, /device:TPU:1, one launch (start us, length us, event | category | flops | bytes accessed | tf_op | source)
XLA Modules:
  0.0 189.6 jit_solution(11986926788099429553)
XLA Ops:
  0.6 186.0 %refit.1 = (bf16[768,128]{1,0:T(8,128)(2,1)}, f32[8,128]{1,0:T(8,128)}, bf16[2304,512]{1,0:T(8,128)(2,1)}, bf16[2304,512]{1,0:T(8,128)(2,1)}, bf16[2048,512]{1,0:T(8,128)(2,1)}) custom-call(bf16[768,128]{1,0:T(8,128)(2,1)} %tokens.1, bf16[128,26624]{1,0:T(8,128)(2,1)} %gate.1, bf16[128,26624]{1,0:T(8,128)(2,1)} %up.1, bf16[26624,128]{1,0:T(8,128)(2,1)} %down.1), custom_call_target="tpu_custom_call" | custom-call | tf_op jit(solution)/shard_map/refit/pallas_call | solution.py:541
  186.7 1.3 slice_reduce_fusion
  188.0 1.6 copy.7

commit v3 on v2

v3 whole, which is shorter than its diff:
```python
import functools

import jax
import jax.numpy as jnp
from jax import lax
from jax.experimental import pallas as pl
from jax.experimental.pallas import tpu as pltpu
from jax.sharding import PartitionSpec as P

MESH = pl.DeviceIdType.MESH
SIDE = 4
SUM_AXES = ((1, 2), (2, 0), (0, 1))


def class_widths(ff):
    units = ff // (8 * 128)
    first = (units + 2) // 3
    second = (units - first + 1) // 2
    return [first * 128, second * 128, (units - first - second) * 128]


def class_bases(widths):
    return [0, 8 * widths[0], 8 * (widths[0] + widths[1])]


def place():
    rep = lax.axis_index("rep")
    tp = lax.axis_index("tp")
    return (rep // SIDE, tp // 2, lax.rem(rep, SIDE)), lax.rem(tp, 2)


def device_at(xyz, core):
    return (xyz[0] * SIDE + xyz[2], xyz[1] * 2 + core)


def moved(xyz, axis, step):
    out = list(xyz)
    out[axis] = lax.rem(xyz[axis] + step, SIDE)
    return tuple(out)


def mult(value, of):
    return pl.multiple_of(value, of)


class Mail:
    def __init__(self, send_sems, recv_sems):
        self.send_sems, self.recv_sems, self.used, self.sent = send_sems, recv_sems, 0, []

    def post(self, src, dst, device):
        copy = pltpu.make_async_remote_copy(
            src_ref=src,
            dst_ref=dst,
            send_sem=self.send_sems.at[self.used],
            recv_sem=self.recv_sems.at[self.used],
            device_id=device,
            device_id_type=MESH,
        )
        self.used += 1
        copy.start()
        self.sent.append(copy)
        return copy

    def settle(self, copies):
        for copy in copies:
            copy.wait_send()
        self.sent = [copy for copy in self.sent if not any(copy is c for c in copies)]

    def finish(self):
        for copy in self.sent:
            copy.wait_send()


def greet(partners):
    for partner in partners:
        pl.semaphore_signal(
            pltpu.get_barrier_semaphore(), inc=1, device_id=partner, device_id_type=MESH
        )


def scale_rows(ref, rows, factor, step=32):
    def body(i, carry):
        at = pl.ds(mult(i * step, step), step)
        wide = ref[at, :].astype(jnp.float32)
        ref[at, :] = jnp.floor(wide * factor + 0.5).astype(jnp.bfloat16)
        return carry

    lax.fori_loop(0, rows // step, body, 0)


def scale_block(ref, rows, col, cols, factor, step=64):
    def body(i, carry):
        at = pl.ds(mult(i * step, step), step)
        wide = ref[at, pl.ds(col, cols)].astype(jnp.float32)
        ref[at, pl.ds(col, cols)] = jnp.floor(wide * factor + 0.5).astype(jnp.bfloat16)
        return carry

    lax.fori_loop(0, rows // step, body, 0)


def kernel(widths, bases, tokens, gate, up, down, *refs):
    refs = list(refs)

    def take(n):
        out = refs[:n]
        del refs[:n]
        return out

    out, peaks_out = take(2)
    down_land = take(3)
    gate_w, up_w, tok, part, near, half, total, far, far_half, hidden, sent, landed = (
        take(3) for _ in range(12)
    )
    acc, blocks, mine_out, peak_send, peak_recv = take(5)
    send_sems, recv_sems, own_sems, load_sems = take(4)
    toks, feat = tokens.shape
    quarter, slab = toks // 4, toks // 16
    mid = quarter // 2
    xyz, core = place()
    other = 1 - core
    mail = Mail(send_sems, recv_sems)

    partners = [device_at(xyz, other)]
    for axis in range(3):
        for step in range(1, SIDE):
            for c in range(2):
                partners.append(device_at(moved(xyz, axis, step), c))
    greet(partners)

    def load(source, spots, first):
        copies = []
        for g in range(3):
            if source is down:
                pieces = 2 * (widths[g] // feat)
            else:
                pieces = 8
            for p in range(pieces):
                if source is down:
                    rows = 4 * feat
                    start = bases[g] + p * rows
                    view = spots[g].at[
                        p % 2, pl.ds(0, rows), pl.ds((p // 2) * feat, feat)
                    ]
                    origin = source.at[pl.ds(start, rows), :]
                else:
                    view = spots[g].at[p // 4, pl.ds((p % 4) * feat, feat), :]
                    origin = source.at[:, pl.ds(bases[g] + p * widths[g], widths[g])]
                copies.append(
                    pltpu.make_async_copy(origin, view, load_sems.at[first + len(copies)])
                )
        for copy in copies:
            copy.start()
        return copies

    def top_of(spots, copies):
        for copy in copies:
            copy.wait()
        best = None
        for g in range(3):

            def body(i, carry, g=g):
                at = pl.ds(mult(i * 32, 32), 32)
                return jnp.maximum(
                    carry, jnp.maximum(jnp.abs(spots[g][0, at, :]), jnp.abs(spots[g][1, at, :]))
                )

            high = lax.fori_loop(
                0, 4 * feat // 32, body, jnp.zeros((32, widths[g]), jnp.bfloat16)
            )
            high = jnp.max(high.astype(jnp.float32))
            best = high if best is None else jnp.maximum(best, high)
        return best

    gate_load = load(gate, part, 0)

    own = {}

    def keep(name, src, dst, sem):
        copy = pltpu.make_async_copy(src, dst, own_sems.at[sem])
        copy.start()
        own[name] = copy

    def token_spot(g, position, c):
        return tok[g].at[:, pl.ds(mult((position * 2 + c) * feat, feat), feat)]

    def weight_spot(kind, g):
        slot = mult((xyz[g] * 2 + core) * feat, feat)
        return (gate_w, up_w)[kind][g].at[pl.ds(slot, feat), pl.ds(0, widths[g])]

    def weight_part(kind, g, position, c):
        col = mult(bases[g] + (position * 2 + c) * widths[g], 128)
        return (gate, up)[kind].at[:, pl.ds(col, widths[g])]

    pl.semaphore_wait(pltpu.get_barrier_semaphore(), len(partners))

    tok_in, tok_rest, tok_cross = ([[], [], []] for _ in range(3))

    def cross_tokens(g, step):
        spot = token_spot(g, lax.rem(xyz[g] + step, SIDE), core)
        tok_cross[g].append(mail.post(spot, spot, device_at(xyz, other)))

    for step in (1, 3):
        for g in range(3):
            there = device_at(moved(xyz, g, step), core)
            tok_in[g].append(mail.post(tokens, token_spot(g, xyz[g], core), there))
    for g in range(3):
        tok_cross[g].append(
            mail.post(tokens, token_spot(g, xyz[g], core), device_at(xyz, other))
        )

    def pass_tokens(g):
        for n, (back, on) in enumerate(((3, 1), (1, 3))):
            tok_in[g][n].wait_recv()
            slot = mult((lax.rem(xyz[g] + back, SIDE) * 2 + core) * feat, feat)
            view = tok[g].at[pl.ds(n * (toks // 2), toks // 2), pl.ds(slot, feat)]
            tok_rest[g].append(mail.post(view, view, device_at(moved(xyz, g, on), core)))
        cross_tokens(g, 3)
        cross_tokens(g, 1)

    weight_in = {}

    def send_weights(kind, step, flip):
        for g in range(3):
            there = moved(xyz, g, step)
            c = core if flip == 0 else other
            weight_in.setdefault((kind, g), []).append(
                mail.post(
                    weight_part(kind, g, there[g], c), weight_spot(kind, g), device_at(there, c)
                )
            )

    send_weights(0, 1, 0)
    send_weights(0, 3, 0)
    up_load = load(up, hidden, 24)
    for g in range(3):
        keep(("tok", g), tokens, token_spot(g, xyz[g], core), g)
        for kind in range(2):
            keep((kind, g), weight_part(kind, g, xyz[g], core), weight_spot(kind, g), 3 + 2 * g + kind)
    gate_top = top_of(part, gate_load)
    down_load = load(down, part, 48)
    up_top = top_of(hidden, up_load)
    down_top = top_of(part, down_load)
    row = lax.broadcasted_iota(jnp.int32, (8, 128), 0)
    tile = jnp.where(row == 0, gate_top, jnp.where(row == 1, up_top, down_top))

    got = 0
    for axis in range(3):
        peak_send[axis] = tile
        waits = []
        for step in range(SIDE):
            for flip in range(2):
                if step == 0 and flip == 0 or axis > 0 and flip == 1:
                    continue
                there = device_at(moved(xyz, axis, step), core if flip == 0 else other)
                waits.append((got, mail.post(peak_send.at[axis], peak_recv.at[got], there)))
                got += 1
        if axis == 0:
            send_weights(0, 1, 1)
            send_weights(0, 3, 1)
        elif axis == 1:
            for g in range(3):
                pass_tokens(g)
            send_weights(0, 2, 0)
        else:
            send_weights(0, 2, 1)
            send_weights(0, 0, 1)
            for flip in range(2):
                for step in (2, 1, 3):
                    send_weights(1, step, flip)
            send_weights(1, 0, 1)
            for g in range(3):
                for copy in tok_rest[g]:
                    copy.wait_recv()
                cross_tokens(g, 2)
        for n, copy in waits:
            copy.wait_recv()
            tile = jnp.maximum(tile, peak_recv[n])
    peaks_out[...] = tile
    factors = [jnp.max(127.0 / tile[k : k + 1, :]) for k in range(3)]
    units = [jnp.max(tile[k : k + 1, :] / 127.0) for k in range(3)]

    def partial_sums(kind, g):
        width = widths[g]
        cols = 384 if width % 384 == 0 else 256 if width % 256 == 0 else 128
        b = xyz[SUM_AXES[g][0]]
        weights = (gate_w, up_w)[kind][g]

        def body(j, carry):
            at = pl.ds(mult(j * cols, 128), cols)
            acc[:, pl.ds(0, cols)] = jnp.dot(
                tok[g][...], weights[pl.ds(0, 8 * feat), at], preferred_element_type=jnp.float32
            )
            part[g][kind, :, at] = acc[:, pl.ds(0, cols)].astype(jnp.bfloat16)
            mine = pl.ds(mult(b * quarter, quarter), quarter)
            total[g][kind, :, at] = acc[mine, pl.ds(0, cols)]
            return carry

        lax.fori_loop(0, width // cols, body, 0)

    def ring_rows(position, size, first, count):
        return pl.ds(mult(position * size + first, 8 if size == slab else 16), count)

    def send_ring(src, whole, piece, axis, kind, size):
        cut = size // 2
        after, before, far_off = (moved(xyz, axis, s) for s in (1, 3, 2))
        pieces = [
            mail.post(
                src.at[kind, ring_rows(far_off[axis], size, n * cut, cut), :],
                piece.at[kind, n],
                device_at(there, core),
            )
            for n, there in enumerate((after, before))
        ]
        wholes = [
            mail.post(
                src.at[kind, ring_rows(there[axis], size, (1 - n) * cut, cut), :],
                whole.at[kind, n, pl.ds((1 - n) * cut, cut), :],
                device_at(there, core),
            )
            for n, there in enumerate((after, before))
        ]
        return pieces, wholes

    def pass_ring(src, whole, piece, axis, kind, size, posts):
        cut = size // 2
        pieces, wholes = posts
        step = 16 if cut % 16 == 0 else 8
        for n, there in enumerate((moved(xyz, axis, 1), moved(xyz, axis, 3))):
            pieces[n].wait_recv()

            def body(i, carry, n=n, there=there):
                at = pl.ds(mult(there[axis] * size + n * cut + i * step, step), step)
                value = src[kind, at, :].astype(jnp.float32) + piece[
                    kind, n, pl.ds(mult(i * step, step), step), :
                ].astype(jnp.float32)
                src[kind, at, :] = value.astype(src.dtype)
                return carry

            lax.fori_loop(0, cut // step, body, 0)
            wholes.append(
                mail.post(
                    src.at[kind, ring_rows(there[axis], size, n * cut, cut), :],
                    whole.at[kind, n, pl.ds(n * cut, cut), :],
                    device_at(there, core),
                )
            )

    down_in = [[], [], []]

    def send_down(step, first, count):
        for g in range(3):
            there = moved(xyz, g, step)
            start = mult(bases[g] + (there[g] * 2 + first) * widths[g], 128)
            down_in[g].append(
                mail.post(
                    down.at[pl.ds(start, count * widths[g]), :],
                    down_land[g].at[step - 1, pl.ds(first * widths[g], count * widths[g]), :],
                    device_at(there, core),
                )
            )

    near_post, far_post = {}, {}
    for kind in range(2):
        for g in range(3):
            for copy in weight_in[kind, g]:
                copy.wait_recv()
            own[kind, g].wait()
            scale_rows((gate_w, up_w)[kind][g], 8 * feat, factors[kind])
            if kind == 0:
                for copy in tok_cross[g]:
                    copy.wait_recv()
                own["tok", g].wait()
            partial_sums(kind, g)
            near_post[kind, g] = send_ring(
                part[g], near[g], half[g], SUM_AXES[g][0], kind, quarter
            )
        if kind == 0:
            send_down(1, 0, 2)
            send_down(3, 0, 2)
    for kind in range(2):
        for g in range(3):
            pass_ring(
                part[g], near[g], half[g], SUM_AXES[g][0], kind, quarter, near_post[kind, g]
            )

    def down_column(g, step, p):
        position = lax.rem(xyz[g] + SIDE - step, SIDE)
        return mult((p * 4 + position) * feat, feat)

    def load_down(g, step):
        for p in range(2):
            if step == 0:
                start = mult(bases[g] + (xyz[g] * 2 + p) * widths[g], 128)
                src = down.at[pl.ds(start, widths[g]), :]
            else:
                src = down_land[g].at[step - 1, pl.ds(p * widths[g], widths[g]), :]
            keep(
                ("down", g, step, p),
                src,
                gate_w[g].at[pl.ds(0, widths[g]), pl.ds(down_column(g, step, p), feat)],
                9 + 8 * g + 2 * step + p,
            )

    def scale_down(g, step):
        for p in range(2):
            own["down", g, step, p].wait()
            scale_block(gate_w[g], widths[g], down_column(g, step, p), feat, factors[2])

    for g in range(3):
        load_down(g, 0)
        for n, step in enumerate((1, 3)):
            down_in[g][n].wait_recv()
            load_down(g, step)
    for g in range(3):
        for step in (0, 1, 3):
            scale_down(g, step)

    for kind in range(2):
        for g in range(3):
            for copy in near_post[kind, g][1]:
                copy.wait_recv()

            def body(i, carry, kind=kind, g=g):
                at = pl.ds(mult(i * 16, 16), 16)
                total[g][kind, at, :] = total[g][kind, at, :] + (
                    near[g][kind, 0, at, :].astype(jnp.float32)
                    + near[g][kind, 1, at, :].astype(jnp.float32)
                )
                return carry

            lax.fori_loop(0, quarter // 16, body, 0)
            far_post[kind, g] = send_ring(
                total[g], far[g], far_half[g], SUM_AXES[g][1], kind, slab
            )
    for kind in range(2):
        for g in range(3):
            pass_ring(
                total[g], far[g], far_half[g], SUM_AXES[g][1], kind, slab, far_post[kind, g]
            )
    send_down(2, 0, 1)

    slab_in = [[], [], []]
    for g in range(3):
        b_axis, c_axis = SUM_AXES[g]
        for kind in range(2):
            for copy in far_post[kind, g][1]:
                copy.wait_recv()
        start = xyz[b_axis] * quarter + xyz[c_axis] * slab

        def body(i, carry, g=g, c_axis=c_axis, start=start):
            at = pl.ds(mult(i * 16, 16), 16)
            mine = pl.ds(mult(xyz[c_axis] * slab + i * 16, 16), 16)
            sums = []
            for kind in range(2):
                value = total[g][kind, mine, :] + (far[g][kind, 0, at, :] + far[g][kind, 1, at, :])
                sums.append(value * units[kind])
            value = sums[0] / (1.0 + jnp.exp(-sums[0])) * sums[1]
            hidden[g][core, pl.ds(mult(start + i * 16, 16), 16), :] = value.astype(jnp.bfloat16)
            return carry

        lax.fori_loop(0, slab // 16, body, 0)
        home = hidden[g].at[core, pl.ds(mult(start, slab), slab), :]
        for step in (2, 1, 3):
            slab_in[g].append(mail.post(home, home, device_at(moved(xyz, c_axis, step), core)))
    send_down(2, 1, 1)

    quarter_in, rest_in, cross_in = [[], [], []], [[], [], []], [[], [], []]

    def hidden_rows(g, step, first, count):
        position = lax.rem(xyz[SUM_AXES[g][0]] + step, SIDE)
        return hidden[g].at[core, ring_rows(position, quarter, first, count), :]

    def cross(g, step):
        view = hidden_rows(g, step, 0, quarter)
        cross_in[g].append(mail.post(view, view, device_at(xyz, other)))

    for g in range(3):
        axis = SUM_AXES[g][0]
        for copy in slab_in[g]:
            copy.wait_recv()
        for first in (0, 1):
            for n, step in enumerate((1, 3)):
                view = hidden_rows(g, 0, mid if first != n else 0, mid)
                quarter_in[g].append(
                    mail.post(view, view, device_at(moved(xyz, axis, step), core))
                )
        cross(g, 0)

    for g in range(3):
        for copy in down_in[g][2:]:
            copy.wait_recv()
        load_down(g, 2)
    mine_out[...] = jnp.zeros_like(mine_out)
    for g in range(3):
        scale_down(g, 2)

    landed_in = {}

    def token_rows(g, step):
        return ring_rows(lax.rem(xyz[SUM_AXES[g][0]] + step, SIDE), quarter, 0, quarter)

    def output_part(g, rows, p):
        return jnp.dot(
            hidden[g][p, rows, :],
            gate_w[g][pl.ds(0, widths[g]), pl.ds(mult(p * 4 * feat, 4 * feat), 4 * feat)],
            preferred_element_type=jnp.float32,
        )

    def output_rows(g, step, value):
        rows = token_rows(g, step)
        for j in range(SIDE):
            block = value[:, j * feat : (j + 1) * feat]
            blocks[j] = block
            sent[g][j, rows, :] = block.astype(jnp.bfloat16)
        mine_out[rows, :] = mine_out[rows, :] + blocks[xyz[g]]
        for move in (2, 1, 3):
            there = moved(xyz, g, move)
            landed_in.setdefault((g, step), []).append(
                mail.post(
                    sent[g].at[there[g], rows, :],
                    landed[g].at[move - 1, rows, :],
                    device_at(there, core),
                )
            )

    def add_landed(g, step):
        for copy in landed_in[g, step]:
            copy.wait_recv()
        rows = token_rows(g, step)
        terms = [landed[g][n, rows, :].astype(jnp.float32) for n in range(3)]
        mine_out[rows, :] = (mine_out[rows, :] + terms[1]) + (terms[0] + terms[2])

    def output_own(step):
        for g in range(3):
            total[g][0, :, pl.ds(0, 4 * feat)] = output_part(g, token_rows(g, step), core)

    def output_rest(n, step):
        for g in range(3):
            cross_in[g][n].wait_recv()
            value = total[g][0, :, pl.ds(0, 4 * feat)] + output_part(g, token_rows(g, step), other)
            output_rows(g, step, value)

    for posts in far_post.values():
        mail.settle(posts[0] + posts[1])
    output_own(0)
    output_rest(0, 0)

    for g in range(3):
        axis = SUM_AXES[g][0]
        for n, (back, on) in enumerate(((3, 1), (1, 3))):
            quarter_in[g][n].wait_recv()
            view = hidden_rows(g, back, n * mid, mid)
            rest_in[g].append(mail.post(view, view, device_at(moved(xyz, axis, on), core)))
    for n, back in enumerate((3, 1)):
        for g in range(3):
            quarter_in[g][2 + n].wait_recv()
            cross(g, back)
    output_own(3)
    output_rest(1, 3)
    output_own(1)
    output_rest(2, 1)
    for g in range(3):
        for copy in rest_in[g]:
            copy.wait_recv()
        cross(g, 2)
    output_own(2)
    for step in (0, 3):
        for g in range(3):
            add_landed(g, step)
    output_rest(3, 2)
    for step in (1, 2):
        for g in range(3):
            add_landed(g, step)
    out[...] = (mine_out[...] * units[2]).astype(jnp.bfloat16)
    mail.finish()


def shards(tokens, gate_weight, up_weight, down_weight):
    toks, feat = tokens.shape
    ff = gate_weight.shape[1]
    widths = class_widths(ff)
    bases = class_bases(widths)
    quarter, slab = toks // 4, toks // 16
    bf16, f32 = jnp.bfloat16, jnp.float32
    hbm = pl.BlockSpec(memory_space=pl.ANY)
    vmem = pl.BlockSpec(memory_space=pltpu.VMEM)
    shape = jax.ShapeDtypeStruct

    scratch = [pltpu.VMEM((max(8 * feat, w), max(8 * feat, w)), bf16) for w in widths]
    scratch += [pltpu.VMEM((8 * feat, w), bf16) for w in widths]
    scratch += [pltpu.VMEM((toks, 8 * feat), bf16) for _ in widths]
    scratch += [pltpu.VMEM((2, toks, w), bf16) for w in widths]
    scratch += [pltpu.VMEM((2, 2, quarter, w), bf16) for w in widths]
    scratch += [pltpu.VMEM((2, 2, quarter // 2, w), bf16) for w in widths]
    scratch += [pltpu.VMEM((2, quarter, w), f32) for w in widths]
    scratch += [pltpu.VMEM((2, 2, slab, w), f32) for w in widths]
    scratch += [pltpu.VMEM((2, 2, slab // 2, w), f32) for w in widths]
    scratch += [pltpu.VMEM((2, toks, w), bf16) for w in widths]
    scratch += [pltpu.VMEM((SIDE, toks, feat), bf16) for _ in widths]
    scratch += [pltpu.VMEM((3, toks, feat), bf16) for _ in widths]
    scratch += [
        pltpu.VMEM((toks, 384), f32),
        pltpu.VMEM((SIDE, quarter, feat), f32),
        pltpu.VMEM((toks, feat), f32),
        pltpu.VMEM((3, 8, 128), f32),
        pltpu.VMEM((13, 8, 128), f32),
        pltpu.SemaphoreType.DMA((238,)),
        pltpu.SemaphoreType.DMA((238,)),
        pltpu.SemaphoreType.DMA((33,)),
        pltpu.SemaphoreType.DMA((100,)),
    ]
    outs = pl.pallas_call(
        functools.partial(kernel, widths, bases),
        out_shape=(
            shape((toks, feat), bf16),
            shape((8, 128), f32),
            *[shape((3, 2 * w, feat), bf16) for w in widths],
        ),
        in_specs=[hbm] * 4,
        out_specs=(vmem, vmem, hbm, hbm, hbm),
        scratch_shapes=scratch,
        compiler_params=pltpu.CompilerParams(
            collective_id=0, has_side_effects=True, vmem_limit_bytes=63 * 2**20
        ),
        name="refit",
    )(tokens, gate_weight, up_weight, down_weight)
    return outs[0], outs[1][:3, 0]


def solution(mesh):
    in_specs = (
        P(None, ("rep", "tp")),
        P(("rep", "tp"), None),
        P(("rep", "tp"), None),
        P(None, ("rep", "tp")),
    )
    out_specs = (P(None, ("rep", "tp")), P())
    return jax.shard_map(shards, mesh=mesh, in_specs=in_specs, out_specs=out_specs, check_vma=False)
```

time: 190 us -> 176 us (0.926)
  Pallas kernels: 186 us -> 172 us
    pallas_call x1, Pallas kernels: 186 us -> 172 us  [shards(): pl.pallas_call(functools.partial(kernel, widths, bases), out_shape=(shape...]
where the time goes in v3:
time: 176 us; the launch traced here: 175 us
  Pallas kernels  172 us (98%)
  local copies, waits for them, and re-layouts  2.91 us (2%)
    pallas_call x1, Pallas kernels, shards(): pl.pallas_call(functools.partial(kernel, widths, bases), out_shape=(shape...  172 us

profile of v3, /device:TPU:1, one launch (start us, length us, event | category | flops | bytes accessed | tf_op | source)
XLA Modules:
  0.0 175.4 jit_solution(13098307834067836987)
XLA Ops:
  0.6 171.9 %refit.1 = (bf16[768,128]{1,0:T(8,128)(2,1)}, f32[8,128]{1,0:T(8,128)}, bf16[3,2304,128]{2,1,0:T(8,128)(2,1)}, bf16[3,2304,128]{2,1,0:T(8,128)(2,1)}, bf16[3,2048,128]{2,1,0:T(8,128)(2,1)}) custom-call(bf16[768,128]{1,0:T(8,128)(2,1)} %tokens.1, bf16[128,26624]{1,0:T(8,128)(2,1)} %gate.1, bf16[128,26624]{1,0:T(8,128)(2,1)} %up.1, bf16[26624,128]{1,0:T(8,128)(2,1)} %down.1), custom_call_target="tpu_custom_call" | custom-call | tf_op jit(solution)/shard_map/refit/pallas_call | solution.py:612
  172.5 1.3 slice_reduce_fusion
  173.8 1.6 copy.7

commit v4 on v3

--- a/solution.py
+++ b/solution.py
@@ -61,11 +61,6 @@
         self.sent.append(copy)
         return copy
 
-    def settle(self, copies):
-        for copy in copies:
-            copy.wait_send()
-        self.sent = [copy for copy in self.sent if not any(copy is c for c in copies)]
-
     def finish(self):
         for copy in self.sent:
             copy.wait_send()
@@ -108,7 +103,7 @@
 
     out, peaks_out = take(2)
     down_land = take(3)
-    gate_w, up_w, tok, part, near, half, total, far, far_half, hidden, sent, landed = (
+    gate_w, up_w, tok, part, near, half, kept, total, far, hidden, sent, landed = (
         take(3) for _ in range(12)
     )
     acc, blocks, mine_out, peak_send, peak_recv = take(5)
@@ -282,7 +277,9 @@
     def partial_sums(kind, g):
         width = widths[g]
         cols = 384 if width % 384 == 0 else 256 if width % 256 == 0 else 128
-        b = xyz[SUM_AXES[g][0]]
+        axis = SUM_AXES[g][0]
+        b = xyz[axis]
+        neighbours = (moved(xyz, axis, 1)[axis], moved(xyz, axis, 3)[axis])
         weights = (gate_w, up_w)[kind][g]
 
         def body(j, carry):
@@ -293,54 +290,55 @@
             part[g][kind, :, at] = acc[:, pl.ds(0, cols)].astype(jnp.bfloat16)
             mine = pl.ds(mult(b * quarter, quarter), quarter)
             total[g][kind, :, at] = acc[mine, pl.ds(0, cols)]
+            for n in range(2):
+                passed = pl.ds(mult(neighbours[n] * quarter + n * mid, mid), mid)
+                kept[g][kind, n, :, at] = acc[passed, pl.ds(0, cols)]
             return carry
 
         lax.fori_loop(0, width // cols, body, 0)
 
-    def ring_rows(position, size, first, count):
-        return pl.ds(mult(position * size + first, 8 if size == slab else 16), count)
-
-    def send_ring(src, whole, piece, axis, kind, size):
-        cut = size // 2
+    def ring_rows(position, first, count):
+        return pl.ds(mult(position * quarter + first, 16), count)
+
+    def send_near(kind, g):
+        axis = SUM_AXES[g][0]
         after, before, far_off = (moved(xyz, axis, s) for s in (1, 3, 2))
         pieces = [
             mail.post(
-                src.at[kind, ring_rows(far_off[axis], size, n * cut, cut), :],
-                piece.at[kind, n],
+                part[g].at[kind, ring_rows(far_off[axis], n * mid, mid), :],
+                half[g].at[kind, n],
                 device_at(there, core),
             )
             for n, there in enumerate((after, before))
         ]
         wholes = [
             mail.post(
-                src.at[kind, ring_rows(there[axis], size, (1 - n) * cut, cut), :],
-                whole.at[kind, n, pl.ds((1 - n) * cut, cut), :],
+                part[g].at[kind, ring_rows(there[axis], (1 - n) * mid, mid), :],
+                near[g].at[kind, n, pl.ds((1 - n) * mid, mid), :],
                 device_at(there, core),
             )
             for n, there in enumerate((after, before))
         ]
         return pieces, wholes
 
-    def pass_ring(src, whole, piece, axis, kind, size, posts):
-        cut = size // 2
+    def pass_near(kind, g, posts):
+        axis = SUM_AXES[g][0]
         pieces, wholes = posts
-        step = 16 if cut % 16 == 0 else 8
         for n, there in enumerate((moved(xyz, axis, 1), moved(xyz, axis, 3))):
             pieces[n].wait_recv()
 
             def body(i, carry, n=n, there=there):
-                at = pl.ds(mult(there[axis] * size + n * cut + i * step, step), step)
-                value = src[kind, at, :].astype(jnp.float32) + piece[
-                    kind, n, pl.ds(mult(i * step, step), step), :
-                ].astype(jnp.float32)
-                src[kind, at, :] = value.astype(src.dtype)
+                local = pl.ds(mult(i * 16, 16), 16)
+                value = kept[g][kind, n, local, :] + half[g][kind, n, local, :].astype(jnp.float32)
+                at = ring_rows(there[axis], n * mid + i * 16, 16)
+                part[g][kind, at, :] = value.astype(jnp.bfloat16)
                 return carry
 
-            lax.fori_loop(0, cut // step, body, 0)
+            lax.fori_loop(0, mid // 16, body, 0)
             wholes.append(
                 mail.post(
-                    src.at[kind, ring_rows(there[axis], size, n * cut, cut), :],
-                    whole.at[kind, n, pl.ds(n * cut, cut), :],
+                    part[g].at[kind, ring_rows(there[axis], n * mid, mid), :],
+                    near[g].at[kind, n, pl.ds(n * mid, mid), :],
                     device_at(there, core),
                 )
             )
@@ -359,7 +357,7 @@
                 )
             )
 
-    near_post, far_post = {}, {}
+    near_post, far_in = {}, [[], [], []]
     for kind in range(2):
         for g in range(3):
             for copy in weight_in[kind, g]:
@@ -371,17 +369,13 @@
                     copy.wait_recv()
                 own["tok", g].wait()
             partial_sums(kind, g)
-            near_post[kind, g] = send_ring(
-                part[g], near[g], half[g], SUM_AXES[g][0], kind, quarter
-            )
+            near_post[kind, g] = send_near(kind, g)
         if kind == 0:
             send_down(1, 0, 2)
             send_down(3, 0, 2)
     for kind in range(2):
         for g in range(3):
-            pass_ring(
-                part[g], near[g], half[g], SUM_AXES[g][0], kind, quarter, near_post[kind, g]
-            )
+            pass_near(kind, g, near_post[kind, g])
 
     def down_column(g, step, p):
         position = lax.rem(xyz[g] + SIDE - step, SIDE)
@@ -420,31 +414,35 @@
             for copy in near_post[kind, g][1]:
                 copy.wait_recv()
 
-            def body(i, carry, kind=kind, g=g):
+            b_axis, c_axis = SUM_AXES[g]
+
+            def body(i, carry, kind=kind, g=g, b_axis=b_axis):
                 at = pl.ds(mult(i * 16, 16), 16)
-                total[g][kind, at, :] = total[g][kind, at, :] + (
+                value = total[g][kind, at, :] + (
                     near[g][kind, 0, at, :].astype(jnp.float32)
                     + near[g][kind, 1, at, :].astype(jnp.float32)
                 )
+                total[g][kind, at, :] = value
+                part[g][kind, ring_rows(xyz[b_axis], i * 16, 16), :] = value.astype(jnp.bfloat16)
                 return carry
 
             lax.fori_loop(0, quarter // 16, body, 0)
-            far_post[kind, g] = send_ring(
-                total[g], far[g], far_half[g], SUM_AXES[g][1], kind, slab
-            )
-    for kind in range(2):
-        for g in range(3):
-            pass_ring(
-                total[g], far[g], far_half[g], SUM_AXES[g][1], kind, slab, far_post[kind, g]
-            )
+            for step in (2, 1, 3):
+                there = moved(xyz, c_axis, step)
+                far_in[g].append(
+                    mail.post(
+                        part[g].at[kind, ring_rows(xyz[b_axis], there[c_axis] * slab, slab), :],
+                        far[g].at[kind, step - 1],
+                        device_at(there, core),
+                    )
+                )
     send_down(2, 0, 1)
 
     slab_in = [[], [], []]
     for g in range(3):
         b_axis, c_axis = SUM_AXES[g]
-        for kind in range(2):
-            for copy in far_post[kind, g][1]:
-                copy.wait_recv()
+        for copy in far_in[g]:
+            copy.wait_recv()
         start = xyz[b_axis] * quarter + xyz[c_axis] * slab
 
         def body(i, carry, g=g, c_axis=c_axis, start=start):
@@ -452,7 +450,8 @@
             mine = pl.ds(mult(xyz[c_axis] * slab + i * 16, 16), 16)
             sums = []
             for kind in range(2):
-                value = total[g][kind, mine, :] + (far[g][kind, 0, at, :] + far[g][kind, 1, at, :])
+                terms = [far[g][kind, n, at, :].astype(jnp.float32) for n in range(3)]
+                value = (total[g][kind, mine, :] + terms[1]) + (terms[0] + terms[2])
                 sums.append(value * units[kind])
             value = sums[0] / (1.0 + jnp.exp(-sums[0])) * sums[1]
             hidden[g][core, pl.ds(mult(start + i * 16, 16), 16), :] = value.astype(jnp.bfloat16)
@@ -468,7 +467,7 @@
 
     def hidden_rows(g, step, first, count):
         position = lax.rem(xyz[SUM_AXES[g][0]] + step, SIDE)
-        return hidden[g].at[core, ring_rows(position, quarter, first, count), :]
+        return hidden[g].at[core, ring_rows(position, first, count), :]
 
     def cross(g, step):
         view = hidden_rows(g, step, 0, quarter)
@@ -497,7 +496,7 @@
     landed_in = {}
 
     def token_rows(g, step):
-        return ring_rows(lax.rem(xyz[SUM_AXES[g][0]] + step, SIDE), quarter, 0, quarter)
+        return ring_rows(lax.rem(xyz[SUM_AXES[g][0]] + step, SIDE), 0, quarter)
 
     def output_part(g, rows, p):
         return jnp.dot(
@@ -540,8 +539,6 @@
             value = total[g][0, :, pl.ds(0, 4 * feat)] + output_part(g, token_rows(g, step), other)
             output_rows(g, step, value)
 
-    for posts in far_post.values():
-        mail.settle(posts[0] + posts[1])
     output_own(0)
     output_rest(0, 0)
 
@@ -592,9 +589,9 @@
     scratch += [pltpu.VMEM((2, toks, w), bf16) for w in widths]
     scratch += [pltpu.VMEM((2, 2, quarter, w), bf16) for w in widths]
     scratch += [pltpu.VMEM((2, 2, quarter // 2, w), bf16) for w in widths]
+    scratch += [pltpu.VMEM((2, 2, quarter // 2, w), f32) for w in widths]
     scratch += [pltpu.VMEM((2, quarter, w), f32) for w in widths]
-    scratch += [pltpu.VMEM((2, 2, slab, w), f32) for w in widths]
-    scratch += [pltpu.VMEM((2, 2, slab // 2, w), f32) for w in widths]
+    scratch += [pltpu.VMEM((2, 3, slab, w), bf16) for w in widths]
     scratch += [pltpu.VMEM((2, toks, w), bf16) for w in widths]
     scratch += [pltpu.VMEM((SIDE, toks, feat), bf16) for _ in widths]
     scratch += [pltpu.VMEM((3, toks, feat), bf16) for _ in widths]
@@ -604,8 +601,8 @@
         pltpu.VMEM((toks, feat), f32),
         pltpu.VMEM((3, 8, 128), f32),
         pltpu.VMEM((13, 8, 128), f32),
-        pltpu.SemaphoreType.DMA((238,)),
-        pltpu.SemaphoreType.DMA((238,)),
+        pltpu.SemaphoreType.DMA((220,)),
+        pltpu.SemaphoreType.DMA((220,)),
         pltpu.SemaphoreType.DMA((33,)),
         pltpu.SemaphoreType.DMA((100,)),
     ]

time: 176 us -> 169 us (0.960)
  Pallas kernels: 172 us -> 166 us
    pallas_call x1, Pallas kernels: 172 us -> 166 us  [shards(): pl.pallas_call(functools.partial(kernel, widths, bases), out_shape=(shape...]
where the time goes in v4:
time: 169 us
  Pallas kernels  166 us (98%)
  local copies, waits for them, and re-layouts  2.91 us (2%)
    pallas_call x1, Pallas kernels, shards(): pl.pallas_call(functools.partial(kernel, widths, bases), out_shape=(shape...  166 us

profile of v4, /device:TPU:1, one launch (start us, length us, event | category | flops | bytes accessed | tf_op | source)
XLA Modules:
  0.0 169.1 jit_solution(7754970563578334306)
XLA Ops:
  0.6 165.6 %refit.1 = (bf16[768,128]{1,0:T(8,128)(2,1)}, f32[8,128]{1,0:T(8,128)}, bf16[3,2304,128]{2,1,0:T(8,128)(2,1)}, bf16[3,2304,128]{2,1,0:T(8,128)(2,1)}, bf16[3,2048,128]{2,1,0:T(8,128)(2,1)}) custom-call(bf16[768,128]{1,0:T(8,128)(2,1)} %tokens.1, bf16[128,26624]{1,0:T(8,128)(2,1)} %gate.1, bf16[128,26624]{1,0:T(8,128)(2,1)} %up.1, bf16[26624,128]{1,0:T(8,128)(2,1)} %down.1), custom_call_target="tpu_custom_call" | custom-call | tf_op jit(solution)/shard_map/refit/pallas_call | solution.py:609
  166.2 1.3 slice_reduce_fusion
  167.5 1.6 copy.7

commit v5 on v4

--- a/solution.py
+++ b/solution.py
@@ -61,8 +61,10 @@
         self.sent.append(copy)
         return copy
 
-    def finish(self):
-        for copy in self.sent:
+    def finish(self, count=None):
+        done = self.sent[:count]
+        self.sent = self.sent[len(done) :]
+        for copy in done:
             copy.wait_send()
 
 
@@ -226,6 +228,8 @@
 
     send_weights(0, 1, 0)
     send_weights(0, 3, 0)
+    send_weights(0, 1, 1)
+    send_weights(0, 3, 1)
     up_load = load(up, hidden, 24)
     for g in range(3):
         keep(("tok", g), tokens, token_spot(g, xyz[g], core), g)
@@ -250,18 +254,18 @@
                 waits.append((got, mail.post(peak_send.at[axis], peak_recv.at[got], there)))
                 got += 1
         if axis == 0:
-            send_weights(0, 1, 1)
-            send_weights(0, 3, 1)
+            send_weights(0, 2, 0)
         elif axis == 1:
             for g in range(3):
                 pass_tokens(g)
-            send_weights(0, 2, 0)
+            send_weights(0, 2, 1)
         else:
-            send_weights(0, 2, 1)
             send_weights(0, 0, 1)
+            for step in (1, 3):
+                for flip in range(2):
+                    send_weights(1, step, flip)
             for flip in range(2):
-                for step in (2, 1, 3):
-                    send_weights(1, step, flip)
+                send_weights(1, 2, flip)
             send_weights(1, 0, 1)
             for g in range(3):
                 for copy in tok_rest[g]:
@@ -270,7 +274,8 @@
         for n, copy in waits:
             copy.wait_recv()
             tile = jnp.maximum(tile, peak_recv[n])
-    peaks_out[...] = tile
+    for k in range(3):
+        peaks_out[k] = jnp.max(tile[k : k + 1, :])
     factors = [jnp.max(127.0 / tile[k : k + 1, :]) for k in range(3)]
     units = [jnp.max(tile[k : k + 1, :] / 127.0) for k in range(3)]
 
@@ -376,6 +381,7 @@
     for kind in range(2):
         for g in range(3):
             pass_near(kind, g, near_post[kind, g])
+    posted = len(mail.sent)
 
     def down_column(g, step, p):
         position = lax.rem(xyz[g] + SIDE - step, SIDE)
@@ -472,6 +478,9 @@
     def cross(g, step):
         view = hidden_rows(g, step, 0, quarter)
         cross_in[g].append(mail.post(view, view, device_at(xyz, other)))
+
+    mail.finish(posted)
+    posted = len(mail.sent)
 
     for g in range(3):
         axis = SUM_AXES[g][0]
@@ -548,6 +557,7 @@
             quarter_in[g][n].wait_recv()
             view = hidden_rows(g, back, n * mid, mid)
             rest_in[g].append(mail.post(view, view, device_at(moved(xyz, axis, on), core)))
+    mail.finish(posted)
     for n, back in enumerate((3, 1)):
         for g in range(3):
             quarter_in[g][2 + n].wait_recv()
@@ -610,18 +620,18 @@
         functools.partial(kernel, widths, bases),
         out_shape=(
             shape((toks, feat), bf16),
-            shape((8, 128), f32),
+            shape((3,), f32),
             *[shape((3, 2 * w, feat), bf16) for w in widths],
         ),
         in_specs=[hbm] * 4,
-        out_specs=(vmem, vmem, hbm, hbm, hbm),
+        out_specs=(vmem, pl.BlockSpec(memory_space=pltpu.SMEM), hbm, hbm, hbm),
         scratch_shapes=scratch,
         compiler_params=pltpu.CompilerParams(
             collective_id=0, has_side_effects=True, vmem_limit_bytes=63 * 2**20
         ),
         name="refit",
     )(tokens, gate_weight, up_weight, down_weight)
-    return outs[0], outs[1][:3, 0]
+    return outs[0], outs[1]
 
 
 def solution(mesh):

time: 169 us -> 169 us (level)
  no operation moved by 1% of the time
where the time goes in v5:
time: 169 us; the launch traced here: 168 us
  Pallas kernels  165 us (98%)
  local copies, waits for them, and re-layouts  2.74 us (2%)
    pallas_call x1, Pallas kernels, shards(): pl.pallas_call(functools.partial(kernel, widths, bases), out_shape=(shape...  165 us

profile of v5, /device:TPU:1, one launch (start us, length us, event | category | flops | bytes accessed | tf_op | source)
XLA Modules:
  0.0 168.5 jit_solution(15763848461583941161)
XLA Ops:
  0.6 165.1 %refit.1 = (bf16[768,128]{1,0:T(8,128)(2,1)}, f32[3]{0:T(128)}, bf16[3,2304,128]{2,1,0:T(8,128)(2,1)}, bf16[3,2304,128]{2,1,0:T(8,128)(2,1)}, bf16[3,2048,128]{2,1,0:T(8,128)(2,1)}) custom-call(bf16[768,128]{1,0:T(8,128)(2,1)} %tokens.1, bf16[128,26624]{1,0:T(8,128)(2,1)} %gate.1, bf16[128,26624]{1,0:T(8,128)(2,1)} %up.1, bf16[26624,128]{1,0:T(8,128)(2,1)} %down.1), custom_call_target="tpu_custom_call" | custom-call | tf_op jit(solution)/shard_map/refit/pallas_call | solution.py:619
  165.7 1.6 copy.8
  167.3 1.1 copy.9
